TPU v7x, 32 devices: a whole 2x2x4 slice. The times are simulated.
32 devices in a mesh: dp: 16 (over z, y, x), mp: 2 (over core).
Axes of the slice: x: 2, y: 2, z: 4, core: 2. Of those that a mesh axis runs over, the one named last changes fastest.
Arguments:
- hidden_in: bfloat16 [8192, 768], P(('dp', 'mp')), may hold values from -6 to 6
- memory: bfloat16 [8192, 768], P(('dp', 'mp')), may hold values from -6 to 6
- output_grad: bfloat16 [8192, 768], P(('dp', 'mp')), may hold values from -6 to 6
- segment_ids: int32 [16, 512], P('dp'), may hold values from 0 to 3, never falling along the last dimension, each value on 1 to 384 neighbouring positions
- route_counts: int32 [16, 16], replicated, may hold values from 0 to 32, as said below
- norm_gains: bfloat16 [3, 768], replicated, may hold values from 0.5 to 1.5
- self_qkv: bfloat16 [3, 768, 768], P(None, None, 'mp'), may hold values from -0.109375 to 0.109375
- self_out: bfloat16 [768, 768], P('mp'), may hold values from -1.75 to 1.75
- cross_qkv: bfloat16 [3, 768, 768], P(None, None, 'mp'), may hold values from -0.109375 to 0.109375
- cross_out: bfloat16 [768, 768], P('mp'), may hold values from -1.75 to 1.75
- ff_in: bfloat16 [768, 3072], P(None, 'mp'), may hold values from -0.21875 to 0.21875
- ff_out: bfloat16 [3072, 768], P('mp'), may hold values from -0.109375 to 0.109375
- rel_bias: bfloat16 [32, 12], P(None, 'mp'), may hold values from -4 to 4
Outputs:
- block_out: bfloat16 [8192, 768], P(('dp', 'mp'))
- input_grad: bfloat16 [8192, 768], P(('dp', 'mp'))
- memory_grad: bfloat16 [8192, 768], P(('dp', 'mp'))
- gains_grad: float32 [3, 768], replicated
- bias_grad: float32 [32, 12], replicated
- self_qkv_grad: float32 [3, 768, 768], P(None, 'dp', 'mp')
- self_out_grad: float32 [768, 768], P('mp', 'dp')
- cross_qkv_grad: float32 [3, 768, 768], P(None, 'dp', 'mp')
- cross_out_grad: float32 [768, 768], P('mp', 'dp')
- ff_in_grad: float32 [768, 3072], P('dp', 'mp')
- ff_out_grad: float32 [3072, 768], P('mp', 'dp')
Inputs may be any that keep to these rules, and one draw needn't show every extreme that they name: route_counts[s, o] is the number of rows that each core of dp index s sends to the same core of dp index o; every row and every column of the table sums to 256. `segment_ids`: each row holds the example ids of one dp index's rows in the owners' layout; they start at 0 and never fall, and each of the 4 examples has 1 to 384 rows.
All inputs are finite; a program needn't handle non-finite values.
Results may differ from a plain program's by a relative error of at most 0.04.
The roundings to bfloat16 on the way count: a program that leaves them out, or rounds other values in their place, can miss the bound.
Values may be sent and summed in bfloat16 or wider, within the bound.
No kernel may reach another device: no remote copies, remote signals or barrier semaphores. Data moves between devices by JAX's collectives and lax.ppermute only.
A program may use at most 128 MiB of HBM per device.

v0:
```python
from functools import partial

import jax
import jax.numpy as jnp
import numpy as np
from jax import lax
from jax.experimental import pallas as pl
from jax.experimental.pallas import tpu as pltpu
from jax.sharding import PartitionSpec as P

HEAD_DIM = 64
MAX_DIST = 128
EPS = 1e-06
MASKED = -1e30
TILE = 256
F32 = jnp.float32
BF16 = jnp.bfloat16
VMEM_LIMIT = 24 * 1024 * 1024
WEIGHT = 3 * 10**10
LIGHT = 10**6
AFTER_SELF = 3 * 10**9
LAST_WEIGHT = 7 * 10**9
FF_FIRST = True
TWO_FIRST = True
FF_STEPS = 3
EXTRA = 8


def bucket_edges(buckets, distance):
    exact_span = buckets // 2
    edge_list = []
    for offset in range(1, 4 * distance):
        if offset < exact_span:
            bucket_now = offset
        else:
            log_ratio = np.log(offset / exact_span) / np.log(distance / exact_span)
            bucket_now = min(buckets - 1, exact_span + int(log_ratio * (buckets - exact_span)))
        while len(edge_list) < bucket_now:
            edge_list.append(offset)
    return np.array(edge_list, dtype=np.int32)


def dot(a, b):
    return jnp.dot(a, b, preferred_element_type=F32)


def dot_nt(a, b):
    return lax.dot_general(a, b, (((1,), (1,)), ((), ())), preferred_element_type=F32)


def dot_tn(a, b):
    return lax.dot_general(a, b, (((0,), (0,)), ((), ())), preferred_element_type=F32)


def rms_scale(values):
    return lax.rsqrt(jnp.mean(values * values, axis=-1, keepdims=True) + EPS)


def norm_back(values, gain_row, upstream):
    scale = rms_scale(values)
    scaled = gain_row * upstream
    back = scale * scaled - values * (
        scale * scale * scale * jnp.mean(scaled * values, axis=-1, keepdims=True)
    )
    return back, upstream * values * scale


class Near:
    def __init__(self, array):
        self.array = array


class Far:
    def __init__(self, array, axis=0, count=1):
        self.array, self.axis, self.count = array, axis, count
        self.shape, self.dtype = array.shape, array.dtype


def part(ref, axis, count, i):
    size = ref.shape[axis] // count
    index = tuple(
        pl.ds(i * size, size) if at == axis else slice(None) for at in range(len(ref.shape))
    )
    return ref.at[index]


class Inbound:
    def __init__(self, ref, copies):
        self.ref, self.copies, self.shape = ref, copies, ref.shape
        self.waiting = set(range(len(copies)))

    def need(self, i):
        if i in self.waiting:
            self.waiting.discard(i)
            self.copies[i].wait()

    def __getitem__(self, index):
        for i in range(len(self.copies)):
            self.need(i)
        return self.ref[index]


class Outbound:
    def __init__(self, ref, copies):
        self.ref, self.copies, self.shape, self.dtype = ref, copies, ref.shape, ref.dtype
        self.pending, self.flying = set(range(len(copies))), set()

    def __getitem__(self, index):
        return self.ref[index]

    def __setitem__(self, index, value):
        self.ref[index] = value

    def flush(self, i=None):
        for at in sorted(self.pending) if i is None else [i]:
            self.pending.discard(at)
            self.flying.add(at)
            self.copies[at].start()

    def end(self):
        self.flush()
        for at in sorted(self.flying):
            self.copies[at].wait()


def need(ref, i):
    if isinstance(ref, Inbound):
        ref.need(i % len(ref.copies))
        return ref.ref
    return ref


def flush(*refs, i=None):
    for ref in refs:
        if isinstance(ref, Outbound):
            ref.flush(i)


def call(body, outs, args, flops=0, scratch=(), smem=(), after=(), weight=WEIGHT):
    count, extra, made = len(args), len(after), len(outs)
    far_in = [i for i in range(count) if isinstance(args[i], Far)]
    far_out = [i for i in range(made) if isinstance(outs[i], Far)]
    arrays = [a.array if isinstance(a, Far) else a for a in args]
    shapes = [o.array if isinstance(o, Far) else o for o in outs]
    size = sum(a.size * a.dtype.itemsize for a in arrays + shapes)
    sems = sum(args[i].count for i in far_in) + sum(outs[i].count for i in far_out)

    given = [
        pltpu.with_memory_space_constraint(a, pltpu.HBM) if i in far_in else a
        for i, a in enumerate(arrays)
    ]

    def kernel(*refs):
        ins, refs = list(refs[:count]), refs[count + extra :]
        to, refs = list(refs[:made]), refs[made:]
        rooms, refs = refs[: len(far_in)], refs[len(far_in) :]
        shelves, rest = refs[: len(far_out)], refs[len(far_out) :]
        if sems:
            sem, rest = rest[0], rest[1:]
        at = 0
        for i, room in zip(far_in, rooms):
            copies = []
            for j in range(args[i].count):
                cut = (args[i].axis, args[i].count, j)
                copies.append(
                    pltpu.make_async_copy(part(ins[i], *cut), part(room, *cut), sem.at[at])
                )
                copies[-1].start()
                at += 1
            ins[i] = Inbound(room, copies)
        for i, shelf in zip(far_out, shelves):
            copies = []
            for j in range(outs[i].count):
                cut = (outs[i].axis, outs[i].count, j)
                copies.append(
                    pltpu.make_async_copy(part(shelf, *cut), part(to[i], *cut), sem.at[at])
                )
                at += 1
            to[i] = Outbound(shelf, copies)
        body(*ins, *to, *rest)
        for i in far_in:
            for j in sorted(ins[i].waiting):
                ins[i].need(j)
        for i in far_out:
            to[i].flush()
        for i in far_out:
            to[i].end()

    hbm, vmem = pl.BlockSpec(memory_space=pltpu.HBM), pl.BlockSpec(memory_space=pltpu.VMEM)
    return pl.pallas_call(
        kernel,
        out_shape=[
            (pltpu.HBM if i in far_out else pltpu.VMEM)(o.shape, o.dtype) for i, o in enumerate(shapes)
        ],
        in_specs=[
            pl.BlockSpec(memory_space=pltpu.SMEM) if i in smem else hbm if i in far_in else vmem
            for i in range(count)
        ]
        + [pl.BlockSpec(memory_space=pl.ANY) if isinstance(a, Near) else hbm for a in after],
        out_specs=[hbm if i in far_out else vmem for i in range(made)],
        scratch_shapes=[pltpu.VMEM(arrays[i].shape, arrays[i].dtype) for i in far_in]
        + [pltpu.VMEM(shapes[i].shape, shapes[i].dtype) for i in far_out]
        + ([pltpu.SemaphoreType.DMA((sems,))] if sems else [])
        + list(scratch),
        compiler_params=pltpu.CompilerParams(vmem_limit_bytes=VMEM_LIMIT),
        cost_estimate=pl.CostEstimate(
            flops=int(weight), bytes_accessed=0, transcendentals=0
        ),
    )(
        *given,
        *(
            a.array if isinstance(a, Near) else pltpu.with_memory_space_constraint(a, pltpu.HBM)
            for a in after
        ),
    )


def shape(dims, dtype):
    return jax.ShapeDtypeStruct(dims, dtype)


def own_rows(core_ref, half):
    return pl.ds(pl.multiple_of(core_ref[0] * half, half), half)


def their_rows(core_ref, half):
    return pl.ds(pl.multiple_of((1 - core_ref[0]) * half, half), half)


def tables_body(
    counts_ref, me_ref, vec_ref, ids_ref, bias_ref, mask_ref, taken_ref, sent_wide_ref, taken_wide_ref
):
    peers = counts_ref.shape[0]
    capacity = taken_ref.shape[1] // peers
    taken_ref[...] = slot_line(lambda s: counts_ref[s, me_ref[0]], peers, capacity)
    stride = capacity + EXTRA
    sent_wide_ref[...] = slot_line(lambda o: counts_ref[me_ref[0], o], peers, stride)
    taken_wide_ref[...] = slot_line(lambda s: counts_ref[s, me_ref[0]], peers, stride)
    heads, rows = bias_ref.shape[0], mask_ref.shape[0]
    row = lax.broadcasted_iota(jnp.int32, (MAX_DIST, 2 * MAX_DIST), 0)
    column = lax.broadcasted_iota(jnp.int32, (MAX_DIST, 2 * MAX_DIST), 1)
    for head in range(heads):
        line = vec_ref[head : head + 1, :]
        near = pltpu.roll(
            jnp.broadcast_to(line, (MAX_DIST, 2 * MAX_DIST)), 0, 1, stride=1, stride_axis=0
        )
        near = jnp.where(column > row + MAX_DIST, MASKED, near)
        far = jnp.broadcast_to(line[:, 2 * MAX_DIST - 1 :], (MAX_DIST, MAX_DIST))
        none = jnp.full((MAX_DIST, MAX_DIST), MASKED, F32)
        upper = jnp.concatenate([far, near, none], axis=1)
        lower = jnp.concatenate([far, far, near], axis=1)
        bias_ref[head] = jnp.concatenate([upper, lower], axis=0).astype(BF16)
    ids = ids_ref[...].astype(F32)
    down = jnp.broadcast_to(ids, (128, rows)).T[:, :1]
    mask_ref[...] = jnp.where(down == ids, 0.0, MASKED)


def slot_line(count_of, peers, capacity):
    lane = lax.broadcasted_iota(jnp.int32, (1, peers * capacity), 1)
    line = jnp.full_like(lane, -1)
    start = jnp.int32(0)
    for peer in range(peers):
        count, within = count_of(peer), lane - peer * capacity
        line = jnp.where((within >= 0) & (within < count), start + within, line)
        start = start + count
    return line


def rows_of(line, rows):
    row = lax.broadcasted_iota(jnp.int32, (rows, line.shape[1]), 0)
    return (line == row).astype(BF16)


def pack_body(counts_ref, me_ref, a_ref, b_ref, packed_ref, sent_ref):
    peers, (half, width) = counts_ref.shape[0], a_ref.shape
    capacity = packed_ref.shape[0] // peers
    sent = slot_line(lambda o: counts_ref[me_ref[0], o], peers, capacity)
    sent_ref[...] = sent
    flush(sent_ref)
    slots = rows_of(sent, half)
    packed_ref[:, :width] = dot_tn(slots, a_ref[...]).astype(BF16)
    packed_ref[:, width:] = dot_tn(slots, b_ref[...]).astype(BF16)


def pack_sum_body(line_ref, a_ref, b_ref, packed_ref, token_ref):
    half = a_ref.shape[0]
    skip = b_ref.shape[0] - half
    token_ref[...] = jnp.zeros_like(token_ref)
    rows = (a_ref[...] + b_ref[skip:].astype(F32)).astype(BF16)
    packed_ref[...] = dot_tn(rows_of(line_ref[...], half), rows).astype(BF16)


def unpack_body(line_ref, packed_ref, rows_ref):
    rows_ref[...] = dot(rows_of(line_ref[...], rows_ref.shape[0]), packed_ref[...]).astype(BF16)


def lane_half(values, which):
    lane = lax.broadcasted_iota(jnp.int32, values.shape, 1)
    keep = (lane < HEAD_DIM) if which == 0 else (lane >= HEAD_DIM)
    return jnp.where(keep, values, jnp.zeros_like(values))


def attend(q_ref, k_ref, v_ref, mask_ref, bias_ref, probs_ref, mix_ref):
    rows, columns = q_ref.shape
    causal = bias_ref is not None
    for pair in range(columns // (2 * HEAD_DIM)):
        lanes = slice(pair * 2 * HEAD_DIM, (pair + 1) * 2 * HEAD_DIM)
        for tile in range(rows // TILE):
            here = slice(tile * TILE, (tile + 1) * TILE)
            reach = (tile + 1) * TILE if causal else rows
            q, k, v = q_ref[here, lanes], k_ref[:reach, lanes], v_ref[:reach, lanes]
            mixed = None
            for which in range(2):
                head = 2 * pair + which
                scores = dot_nt(lane_half(q, which), k) + mask_ref[here, :reach]
                if causal:
                    bias = need(bias_ref, head)[head, :, rows - reach :]
                    scores = scores + bias.astype(F32)
                peak = jnp.max(scores, axis=-1, keepdims=True)
                weights = jnp.exp(scores - peak)
                total = jnp.sum(weights, axis=-1, keepdims=True)
                probs = (weights * (1.0 / total)).astype(BF16)
                probs_ref[head, here, :reach] = probs
                each = dot(probs, lane_half(v, which))
                mixed = each if mixed is None else mixed + each
            mix_ref[here, lanes] = mixed.astype(BF16)
        flush(probs_ref, i=2 * pair)
        flush(probs_ref, i=2 * pair + 1)
    flush(mix_ref)


def attend_back(
    q_ref, k_ref, v_ref, probs_ref, d_mix_ref, dq_ref, dk_ref, dv_ref, diag_ref, causal
):
    rows, columns = q_ref.shape
    for pair in range(columns // (2 * HEAD_DIM)):
        lanes = slice(pair * 2 * HEAD_DIM, (pair + 1) * 2 * HEAD_DIM)
        q_turned = q_ref[:, lanes].T
        d_turned = d_mix_ref[:, lanes].T
        dk_turned, dv_turned = [], []
        near = [None, None]
        for which in range(2):
            head = 2 * pair + which
            halves = slice(which * HEAD_DIM, (which + 1) * HEAD_DIM)
            dk_sum = dv_sum = None
            grown = None
            for tile in reversed(range(rows // TILE)):
                here = slice(tile * TILE, (tile + 1) * TILE)
                reach = (tile + 1) * TILE if causal else rows
                k, v = k_ref[:reach, lanes], v_ref[:reach, lanes]
                probs16 = need(probs_ref, head)[head, here, :reach]
                probs = probs16.astype(F32)
                d_probs = dot_nt(lane_half(d_mix_ref[here, lanes], which), v)
                product = probs * d_probs
                delta = jnp.sum(product, axis=-1, keepdims=True)
                d_scores = product - probs * delta
                d_scores16 = d_scores.astype(BF16)
                dq = dot(d_scores16, lane_half(k, which))
                if which == 0:
                    near[tile] = dq
                else:
                    dq_ref[here, lanes] = (near[tile] + dq).astype(BF16)
                dk = dot(q_turned[halves, here], d_scores16)
                dv = dot(d_turned[halves, here], probs16)
                if causal and reach < rows:
                    pad = jnp.zeros((HEAD_DIM, rows - reach), F32)
                    dk = jnp.concatenate([dk, pad], axis=1)
                    dv = jnp.concatenate([dv, pad], axis=1)
                dk_sum = dk if dk_sum is None else dk_sum + dk
                dv_sum = dv if dv_sum is None else dv_sum + dv
                if causal:
                    kept = d_scores16.astype(F32)
                    if reach < rows:
                        kept = jnp.concatenate(
                            [jnp.zeros((TILE, rows - reach), F32), kept], axis=1
                        )
                    grown = kept if grown is None else grown + kept
            dk_turned.append(dk_sum)
            dv_turned.append(dv_sum)
            if causal:
                d = MAX_DIST
                close = grown[:d, d : 3 * d] + grown[d:, 2 * d :]
                row = lax.broadcasted_iota(jnp.int32, close.shape, 0)
                turned, shift = close, 1
                while shift < d:
                    moved = pltpu.roll(turned, 2 * d - shift, 1)
                    turned = jnp.where((row & shift) > 0, moved, turned)
                    shift *= 2
                far = jnp.sum(grown[:d, :d] + grown[d:, :d] + grown[d:, d : 2 * d], axis=0)
                line = jnp.sum(turned, axis=0, keepdims=True)
                spread = jnp.concatenate([line, far[None]], axis=1)
                diag_ref[head] = jnp.broadcast_to(spread, (8, 3 * d))
        dk_ref[:, lanes] = jnp.concatenate(dk_turned, axis=0).T.astype(BF16)
        dv_ref[:, lanes] = jnp.concatenate(dv_turned, axis=0).T.astype(BF16)


def self_forward_body(
    core_ref, own_ref, other_ref, gain_ref, w_ref, mask_ref, bias_ref, wo_ref,
    x_ref, nt_ref, q_ref, k_ref, v_ref, probs_ref, mix_ref, part_ref, n_ref,
):
    half, width = own_ref.shape[0], gain_ref.shape[1]
    x_ref[own_rows(core_ref, half), :] = own_ref[:, :width]
    x_ref[their_rows(core_ref, half), :] = other_ref[:, :width]
    flush(x_ref)
    x = x_ref[...].astype(F32)
    n_ref[...] = (x * rms_scale(x) * gain_ref[...]).astype(BF16)
    for i, out in enumerate((q_ref, k_ref, v_ref)):
        out[...] = dot(n_ref[...], need(w_ref, i)[i]).astype(BF16)
    nt_ref[...] = n_ref[...].T
    flush(q_ref, k_ref, v_ref, nt_ref)
    attend(q_ref, k_ref, v_ref, mask_ref, bias_ref, probs_ref, mix_ref)
    part_ref[...] = dot(mix_ref[...], wo_ref[...]).astype(BF16)


def keys_body(core_ref, own_ref, other_ref, w_ref, k_ref, v_ref, memt_ref, mem_ref):
    half, width = own_ref.shape[0], w_ref.shape[1]
    mem_ref[own_rows(core_ref, half), :] = own_ref[:, width:]
    mem_ref[their_rows(core_ref, half), :] = other_ref[:, width:]
    for i, out in ((1, k_ref), (2, v_ref)):
        out[...] = dot(mem_ref[...], need(w_ref, i)[i]).astype(BF16)
    memt_ref[...] = mem_ref[...].T


def cross_forward_body(
    a_ref, b_ref, x_ref, gain_ref, w_ref, k_ref, mask_ref, v_ref, wo_ref,
    h_ref, h_far_ref, nt_ref, q_ref, probs_ref, mix_ref, part_ref, n_ref,
):
    h_ref[...] = x_ref[...].astype(F32) + (a_ref[...].astype(F32) + b_ref[...].astype(F32))
    h_far_ref[...] = h_ref[...]
    flush(h_far_ref)
    h = h_ref[...]
    n_ref[...] = (h * rms_scale(h) * gain_ref[...]).astype(BF16)
    q_ref[...] = dot(n_ref[...], need(w_ref, 0)[0]).astype(BF16)
    nt_ref[...] = n_ref[...].T
    flush(q_ref, nt_ref)
    attend(q_ref, k_ref, v_ref, mask_ref, None, probs_ref, mix_ref)
    part_ref[...] = dot(mix_ref[...], wo_ref[...]).astype(BF16)


def gelu_pair(v):
    scale = float(np.sqrt(2 / np.pi))
    square = v * v
    t = jnp.tanh(scale * (v + 0.044715 * (square * v)))
    half = 0.5 * (1.0 + t)
    slope = half + 0.5 * v * (1.0 - t * t) * (scale * (1.0 + 3 * 0.044715 * square))
    return v * half, slope


def ff_body(
    core_ref, a_ref, b_ref, h_ref, gain_ref, win_ref, og_ref, wout_ref,
    nt_ref, h2_ref, act_ref, d_pre_ref, base_ref, both_ref, out_sum, back_sum, n_ref,
):
    rows, half = h_ref.shape[0], h_ref.shape[0] // 2
    h = h_ref[...] + (a_ref[...].astype(F32) + b_ref[...].astype(F32))
    h2_ref[...] = h
    n_ref[...] = (h * rms_scale(h) * gain_ref[...]).astype(BF16)
    nt_ref[...] = n_ref[...].T
    steps = FF_STEPS
    block = win_ref.shape[1] // steps
    for step in range(steps):
        units = slice(step * block, (step + 1) * block)
        win, wout = need(win_ref, step), need(wout_ref, step)
        value, slope = gelu_pair(dot(n_ref[...], win[:, units]))
        act_ref[:, units] = value.astype(BF16)
        d_act = dot_nt(og_ref[...], wout[units, :])
        d_pre_ref[:, units] = (d_act * slope).astype(BF16)
        out = dot(act_ref[:, units], wout[units, :])
        back = dot_nt(d_pre_ref[:, units], win[:, units])
        if step:
            out, back = out_sum[...] + out, back_sum[...] + back
        out_sum[...] = out
        if step < steps - 1:
            back_sum[...] = back
        else:
            both_ref[:rows] = back.astype(BF16)
    own, theirs = own_rows(core_ref, half), their_rows(core_ref, half)
    both_ref[rows:] = out_sum[theirs, :].astype(BF16)
    base_ref[...] = h2_ref[own, :] + out_sum[own, :]


def gain_sum(core_ref, dgain):
    row = lax.broadcasted_iota(jnp.int32, dgain.shape, 0)
    half = dgain.shape[0] // 2
    mine = (row >= core_ref[0] * half) & (row < (core_ref[0] + 1) * half)
    return jnp.sum(jnp.where(mine, dgain, 0.0), axis=0, keepdims=True)


def cross_back_body(
    core_ref, a_ref, b_ref, h_ref, up_ref, gain_ref, wo_ref, v_ref, probs_ref, k_ref, q_ref,
    w_ref, base_ref,
    g_ref, gt_ref, dq_ref, dk_ref, dv_ref, both_ref, dmem_ref, dgain_ref, out_ref,
    d_mix_ref, dmem_sum, g16_ref,
):
    rows, half = h_ref.shape[0], h_ref.shape[0] // 2
    up = a_ref[:rows].astype(F32) + b_ref[:rows].astype(F32)
    dv, dgain = norm_back(h_ref[...], gain_ref[...], up)
    dgain_ref[...] = gain_sum(core_ref, dgain)
    g = up_ref[...].astype(F32) + dv
    g_ref[...] = g
    g16_ref[...] = g.astype(BF16)
    d_mix_ref[...] = dot_nt(g16_ref[...], wo_ref[...]).astype(BF16)
    gt_ref[...] = g16_ref[...].T
    attend_back(
        q_ref, k_ref, v_ref, probs_ref, d_mix_ref, dq_ref, dk_ref, dv_ref, None, False
    )
    both_ref[:rows] = dot_nt(dq_ref[...], w_ref[0]).astype(BF16)
    dmem_sum[...] = dot_nt(dk_ref[...], w_ref[1]) + dot_nt(dv_ref[...], w_ref[2])
    both_ref[rows:] = dmem_sum[their_rows(core_ref, half), :].astype(BF16)
    dmem_ref[...] = dmem_sum[own_rows(core_ref, half), :]
    out_ref[...] = (base_ref[...] + b_ref[rows:].astype(F32)).astype(BF16)


def self_back_body(
    core_ref, a_ref, b_ref, h_ref, up_ref, gain_ref, wo_ref, v_ref, probs_ref, k_ref, q_ref, w_ref,
    g_ref, gt_ref, dq_ref, dk_ref, dv_ref, dn_ref, sent_ref, dgain_ref, diag_ref,
    d_mix_ref, total, g16_ref,
):
    rows, half = h_ref.shape[0], h_ref.shape[0] // 2
    own, theirs = own_rows(core_ref, half), their_rows(core_ref, half)
    up = a_ref[:rows].astype(F32) + b_ref[:rows].astype(F32)
    dv, dgain = norm_back(h_ref[...], gain_ref[...], up)
    dgain_ref[...] = gain_sum(core_ref, dgain)
    total[...] = up_ref[...] + dv
    g_ref[...] = total[own, :]
    g16_ref[...] = total[...].astype(BF16)
    d_mix_ref[...] = dot_nt(g16_ref[...], wo_ref[...]).astype(BF16)
    gt_ref[...] = g16_ref[...].T
    attend_back(
        q_ref, k_ref, v_ref, probs_ref, d_mix_ref, dq_ref, dk_ref, dv_ref, diag_ref, True
    )
    total[...] = (
        dot_nt(dq_ref[...], w_ref[0]) + dot_nt(dk_ref[...], w_ref[1]) + dot_nt(dv_ref[...], w_ref[2])
    )
    sent_ref[...] = total[theirs, :].astype(BF16)
    dn_ref[...] = total[own, :]


def extra_slots(count, peers, stride, place):
    lane = lax.broadcasted_iota(jnp.int32, (count, peers * stride), 1)
    row = lax.broadcasted_iota(jnp.int32, (count, peers * stride), 0)
    hot = lane < 0
    for peer in range(peers):
        hot = hot | (lane == peer * stride + place + row)
    return hot.astype(BF16)


def last_body(
    peers, core_ref, line_ref, b_ref, a_ref, x_ref, gain_ref, g_ref, two_ref, three_ref, diag_ref,
    hot_ref, packed_ref,
):
    half, width = b_ref.shape
    x = need(x_ref, 0)[own_rows(core_ref, half), :].astype(F32)
    dv, dgain = norm_back(x, gain_ref[...], a_ref[...] + b_ref[...].astype(F32))
    rows = (g_ref[...] + dv).astype(BF16)
    heads, buckets = diag_ref.shape[0], hot_ref.shape[1]
    lines = jnp.concatenate([diag_ref[head][:1] for head in range(heads)], axis=0)
    sums = jnp.dot(lines, hot_ref[...], preferred_element_type=F32, precision=lax.Precision.HIGHEST)
    twice = jnp.concatenate([sums, sums], axis=1)
    lane = lax.broadcasted_iota(jnp.int32, twice.shape, 1)
    first = core_ref[0] * buckets
    twice = jnp.where((lane >= first) & (lane < first + buckets), twice, 0.0)
    bias = [twice[head : head + 1] for head in range(heads)]
    bias.append(jnp.zeros((1, width - 2 * heads * buckets), F32))
    small = jnp.concatenate(
        [
            jnp.sum(dgain, axis=0, keepdims=True), two_ref[...], three_ref[...],
            jnp.concatenate(bias, axis=1),
        ],
        axis=0,
    )
    high = small.astype(BF16)
    low = (small - high.astype(F32)).astype(BF16)
    small = jnp.concatenate([high, low, jnp.zeros((8, width), BF16)], axis=0)
    stride = packed_ref.shape[0] // peers
    extra = extra_slots(16, peers, stride, stride - EXTRA)
    extra = jnp.where(lax.broadcasted_iota(jnp.int32, extra.shape, 0) < EXTRA, extra, 0.0).astype(BF16)
    packed_ref[...] = (
        dot_tn(rows_of(line_ref[...], half), rows) + dot_tn(extra, small)
    ).astype(BF16)


def unpack_last_body(peers, line_ref, packed_ref, rows_ref, small_ref):
    stride = packed_ref.shape[0] // peers
    rows_ref[...] = dot(rows_of(line_ref[...], rows_ref.shape[0]), packed_ref[...]).astype(BF16)
    flush(rows_ref)
    halves = dot(extra_slots(8, peers, stride, stride - EXTRA), packed_ref[...])
    small_ref[...] = jnp.concatenate(
        [halves[:4] + halves[4:], jnp.zeros((4, small_ref.shape[1]), F32)], axis=0
    )


def grads_in_body(core_ref, own_ref, other_ref, og_ref, turned_ref):
    half = own_ref.shape[0]
    og_ref[own_rows(core_ref, half), :] = own_ref[...]
    og_ref[their_rows(core_ref, half), :] = other_ref[...]
    turned_ref[...] = og_ref[...].T


def relative_block(order, place):
    steps = len(order)
    return sum(((place >> (steps - 1 - at)) & 1) << bit for at, bit in enumerate(order))


def weights_into(plan, peers, me_ref, refs, outs):
    for side, (order, steps) in enumerate(plan):
        keep, send = outs[2 * side], outs[2 * side + 1]
        at = 0
        for left, rights in steps:
            width = refs[left].shape[0]
            size = width // peers

            def rows(first, last):
                ref = need(refs[left], 0)
                if order is None:
                    return ref[first * size : last * size, :]
                blocks = [
                    ref[pl.ds(pl.multiple_of((relative_block(order, p) ^ me_ref[0]) * size, size), size), :]
                    for p in range(first, last)
                ]
                return jnp.concatenate(blocks, axis=0)

            for out, left_rows in ((send, rows(peers // 2, peers)), (keep, rows(0, peers // 2))):
                edge = at
                for right, low, high in rights:
                    out[: width // 2, edge : edge + high - low] = dot(
                        left_rows, refs[right][:, low:high]
                    ).astype(BF16)
                    edge += high - low
            at = edge
        flush(keep)


def weight_body(plan, peers, me_ref, *refs):
    weights_into(plan, peers, me_ref, refs, refs[-2 * len(plan) :])


def split_sum(kept, arrived, keep, send, columns=slice(None), skip=0):
    half = kept.shape[0] // 2
    send[skip : skip + half, columns] = (kept[half:].astype(F32) + arrived[half:].astype(F32)).astype(BF16)
    keep[:, columns] = (kept[:half].astype(F32) + arrived[:half].astype(F32)).astype(BF16)


def weight_add_body(plan, peers, me_ref, *refs):
    keep_a, send_x, keep_b, send_y, keep_ca, keep_cb = refs[-6:]
    ca, from_x, cb, from_y = refs[-10:-6]
    weights_into(plan, peers, me_ref, refs, [keep_a, send_x, keep_b, send_y])
    skip = keep_a.shape[0]
    split_sum(need(ca, 0)[...], from_x[...], keep_ca, send_y, skip=skip)
    split_sum(need(cb, 0)[...], from_y[...], keep_cb, send_x, skip=skip)


def add_both_body(
    sa, sb, ca, cb, from_x, from_y,
    keep_sa, keep_sb, send_x, send_y, keep_c, send_z,
):
    skip, wide = sa.shape[0], ca.shape[1]
    split_sum(sa[...], from_x[:skip], keep_sa, send_y)
    split_sum(sb[...], from_y[:skip], keep_sb, send_x)
    split_sum(ca[...], from_y[skip:], keep_c, send_z, slice(0, wide))
    split_sum(cb[...], from_x[skip:], keep_c, send_z, slice(wide, 2 * wide))


def add_last_body(sa, sb, c, from_x, from_y, from_z, keep_s, send_z, keep_c, send_w):
    wide = sa.shape[1]
    split_sum(sa[...], from_y[...], keep_s, send_z, slice(0, wide))
    split_sum(sb[...], from_x[...], keep_s, send_z, slice(wide, 2 * wide))
    split_sum(c[...], from_z[...], keep_c, send_w)


def weight_halves(me, peers, orders, sides, after=(), weight=WEIGHT, also=None):
    args, plan, outs = [me], [], []
    flops = 0

    def place(array):
        far = isinstance(array, Far)
        for i, known in enumerate(args):
            if known is array or (far and isinstance(known, Far) and known.array is array.array):
                return i
        args.append(array)
        return len(args) - 1

    for order, side in zip(orders, sides):
        steps, total = [], 0
        for left, rights in side:
            width, rows = left.shape
            if (width // peers) % 16:
                array = left.array if isinstance(left, Far) else left
                blocks = np.array([relative_block(order, p) for p in range(peers)])
                index = (blocks ^ me[0])[:, None] * (width // peers) + np.arange(width // peers)
                left = jnp.take(array, index.reshape(-1), axis=0)
                order_here = None
            else:
                order_here = order
            steps.append((
                place(left) - 1,
                tuple((place(right) - 1, low, high) for right, low, high in rights),
            ))
            columns = sum(high - low for _, low, high in rights)
            total += columns
            flops += 2 * rows * width * columns
        plan.append((order_here, tuple(steps)))
        outs += pieces(width // 2, total)
    body = weight_body
    if also is not None:
        body = weight_add_body
        args += also
        keep_a, send_a, keep_b, send_b = outs
        tall = shape((width // 2 + also[0].shape[0] // 2, total), BF16)
        small = Far(shape((also[0].shape[0] // 2, also[0].shape[1]), BF16))
        outs = [keep_a, tall, keep_b, tall, small, small]
    return call(
        partial(body, tuple(plan), peers), outs, args, flops=flops, smem=(0,),
        after=after, weight=weight,
    )


def add_split_body(*refs):
    count = len(refs) // 4
    for i in range(count):
        kept, arrived = refs[2 * i], refs[2 * i + 1]
        keep, send = refs[2 * count + 2 * i], refs[2 * count + 2 * i + 1]
        half = keep.shape[0]
        send[...] = (kept[half:].astype(F32) + arrived[half:].astype(F32)).astype(BF16)
        flush(send)
        keep[...] = (kept[:half].astype(F32) + arrived[:half].astype(F32)).astype(BF16)
        flush(keep)


def add_join_body(*refs):
    keep, send = refs[-2:]
    half, at = keep.shape[0], 0
    for i in range(len(refs) // 2 - 1):
        kept, arrived = refs[2 * i], refs[2 * i + 1]
        columns = slice(at, at + kept.shape[1])
        at += kept.shape[1]
        send[:, columns] = (kept[half:].astype(F32) + arrived[half:].astype(F32)).astype(BF16)
        keep[:, columns] = (kept[:half].astype(F32) + arrived[:half].astype(F32)).astype(BF16)


def finish_body(moves, kept_ref, arrived_ref, *outs):
    total = kept_ref[...].astype(F32) + arrived_ref[...].astype(F32)
    for out, index, spans in moves:
        at = 0
        for low, high in spans:
            part = total[:, low:high]
            edge = at + high - low
            if index is None:
                outs[out][:, at:edge] = part
            else:
                outs[out][index, :, at:edge] = part
            at = edge


def exchange_rows(packed, peers):
    dims = packed.shape
    blocks = packed.reshape(peers, dims[0] // peers, dims[1])
    return lax.all_to_all(blocks, "dp", split_axis=0, concat_axis=0, tiled=True).reshape(dims)


def swap(values):
    return lax.ppermute(values, "mp", [(0, 1), (1, 0)])


def neighbour(values, bit, peers):
    return lax.ppermute(values, "dp", [(i, i ^ (1 << bit)) for i in range(peers)])


def pieces(rows, *columns):
    return [kind(shape((rows, n), BF16)) for n in columns for kind in (Far, lambda s: s)]


class Sum:
    def __init__(self, halves, orders, peers):
        self.halves, self.orders, self.peers, self.place = halves, orders, peers, 0
        self.send()

    def send(self):
        self.arrived = [
            neighbour(self.halves[2 * i + 1], order[self.place], self.peers)
            for i, order in enumerate(self.orders[: len(self.halves) // 2])
        ]
        self.place += 1

    def pairs(self):
        return [
            a for i, got in enumerate(self.arrived) for a in (self.halves[2 * i], got)
        ]

    def step(self, after=()):
        kept = self.halves[0::2]
        half = kept[0].shape[0] // 2
        if half % 16:
            total = (kept[0].astype(F32) + self.arrived[0].astype(F32)).astype(BF16)
            self.halves = [total[:half], total[half:]]
        elif self.place < len(self.orders) or len(kept) == 1:
            outs = pieces(half, *(k.shape[1] for k in kept))
            self.halves = call(add_split_body, outs, self.pairs(), after=after, weight=LIGHT)
        else:
            outs = pieces(half, sum(k.shape[1] for k in kept))
            self.halves = call(add_join_body, outs, self.pairs(), after=after, weight=LIGHT)
        self.send()
        return self.halves[0]

    def finish(self, outs, moves, after=(), weight=LIGHT):
        while self.place < len(self.orders[0]):
            self.step()
        return call(
            partial(finish_body, moves), [Far(o) for o in outs], self.pairs(), after=after, weight=weight
        )


def local(
    hidden_in,
    memory,
    output_grad,
    segment_ids,
    route_counts,
    norm_gains,
    self_qkv,
    self_out,
    cross_qkv,
    cross_out,
    ff_in,
    ff_out,
    rel_bias,
):
    peers = lax.axis_size("dp")
    me = lax.axis_index("dp")
    core = lax.axis_index("mp")
    core_ref = core.astype(jnp.int32)[None]
    half_rows, width = hidden_in.shape
    rows = 2 * half_rows
    capacity = 2 * (half_rows // peers)
    buckets, heads = rel_bias.shape
    columns = self_out.shape[0]
    units = ff_out.shape[0]
    block = width // peers
    bits = peers.bit_length() - 1
    rest = tuple(range(3, bits))
    orders = ((0, 1, 2) + rest, (1, 2, 0) + rest, (2, 0, 1) + rest)
    pair_orders = ((0, 1, 2) + rest, (1, 0, 2) + rest)
    me_ref = me.astype(jnp.int32)[None]
    slots = peers * capacity
    wide, narrow = shape((rows, width), BF16), shape((rows, columns), BF16)
    wide32, gain_shape = shape((rows, width), F32), shape((1, width), F32)
    half16, half32 = shape((half_rows, width), BF16), shape((half_rows, width), F32)
    more16 = shape((rows + half_rows, width), BF16)
    turned = shape((width, rows), BF16)
    probs_shape = shape((heads, rows, rows), BF16)
    square = rows * width * columns
    scores = heads * rows * rows

    packed, sent = call(
        pack_body,
        [shape((slots, 2 * width), BF16), Far(shape((1, slots), jnp.int32))],
        [route_counts, me_ref, Far(hidden_in), Far(memory)],
        smem=(0, 1),
    )
    arrived = exchange_rows(packed, peers)

    gains = norm_gains.astype(F32)
    gain_one, gain_two, gain_three = gains[0:1], gains[1:2], gains[2:3]
    edges = bucket_edges(buckets, MAX_DIST)
    offset = MAX_DIST - np.arange(3 * MAX_DIST)
    bucket_of = np.where(
        (offset >= 0), np.searchsorted(edges, offset, side="right"), buckets - 1
    )
    bucket_hot = bucket_of[:, None] == np.arange(buckets)[None, :]
    lines = jnp.dot(
        bucket_hot[: 2 * MAX_DIST].astype(jnp.bfloat16), rel_bias, preferred_element_type=F32
    ).T
    line = Far(shape((1, slots), jnp.int32))
    line_wide = Far(shape((1, slots + peers * EXTRA), jnp.int32))
    bias, mask, taken, sent_wide, taken_wide = call(
        tables_body,
        [
            Far(shape((heads, TILE, rows), BF16)), Far(shape((rows, rows), F32)), line, line_wide,
            line_wide,
        ],
        [route_counts, me_ref, lines, segment_ids],
        smem=(0, 1),
        after=[sent],
    )
    og, og_turned = call(
        grads_in_body,
        [Far(wide), Far(turned)],
        [core_ref, output_grad, swap(output_grad)],
        smem=(0,),
        after=[mask],
    )
    [own] = call(
        unpack_body,
        [shape((half_rows, 2 * width), BF16)],
        [taken, arrived],
        after=[mask, og_turned],
    )
    other = swap(own)

    by_head = partial(Far, axis=0, count=heads)
    x, n1_turned, sq, sk, sv, self_probs, self_mix, part_one = call(
        self_forward_body,
        [
            Far(wide), Far(turned), Far(narrow), Far(narrow), Far(narrow), by_head(probs_shape),
            Far(narrow), wide,
        ],
        [core_ref, own, other, gain_one, self_qkv, mask, bias, self_out],
        flops=8 * square + 8 * scores * HEAD_DIM,
        scratch=[pltpu.VMEM((rows, width), BF16)],
        smem=(0,),
    )
    part_there = swap(part_one)
    ck, cv, mem_turned = call(
        keys_body,
        [narrow, narrow, Far(turned)],
        [core_ref, own, other, cross_qkv],
        flops=4 * square,
        scratch=[pltpu.VMEM((rows, width), BF16)],
        smem=(0,),
        after=[x],
    )
    h1, h1_far, n2_turned, cq, cross_probs, cross_mix, part_two = call(
        cross_forward_body,
        [wide32, Far(wide32), Far(turned), Far(narrow), by_head(probs_shape), Far(narrow), wide],
        [part_one, part_there, Far(x), gain_two, cross_qkv, ck, mask, cv, cross_out],
        flops=4 * square + 8 * scores * HEAD_DIM,
        scratch=[pltpu.VMEM((rows, width), BF16)],
    )
    n3_turned, h2, act, d_pre, base, pack3 = call(
        ff_body,
        [turned, wide32, shape((rows, units), BF16), shape((rows, units), BF16), half32, more16],
        [core_ref, part_two, swap(part_two), h1, gain_three, ff_in, og, ff_out],
        flops=8 * rows * width * units,
        scratch=[
            pltpu.VMEM((rows, width), F32), pltpu.VMEM((rows, width), F32),
            pltpu.VMEM((rows, width), BF16),
        ],
        smem=(0,),
    )
    pack3_there = swap(pack3)

    third = 2 * units // 3
    ff_sum = Sum(
        weight_halves(me_ref, peers, orders, [
            [(Far(og_turned), [(act, 0, third)])],
            [
                (Far(og_turned), [(act, third, units)]),
                (n3_turned, [(d_pre, 0, 2 * third - units)]),
            ],
            [(n3_turned, [(d_pre, 2 * third - units, units)])],
        ]),
        orders, peers,
    )
    g2, g2_turned, dcq, dck, dcv, pack2, d_mem, dgain3, block_out = call(
        cross_back_body,
        [
            Far(wide32), turned, narrow, narrow, narrow, Far(more16), half32, Far(gain_shape), Far(half16),
        ],
        [
            core_ref, pack3, pack3_there, h2, og, gain_three, cross_out, cv,
            cross_probs, ck, cq, cross_qkv, base,
        ],
        flops=8 * square + 14 * scores * HEAD_DIM,
        scratch=[
            pltpu.VMEM((rows, columns), BF16), pltpu.VMEM((rows, width), F32),
            pltpu.VMEM((rows, width), BF16),
        ],
        smem=(0,),
        after=[ff_sum.halves[0]],
    )
    pack2_there = swap(pack2)
    cross_sum = Sum(
        weight_halves(me_ref, peers, pair_orders, [
            [(g2_turned, [(cross_mix, 0, columns)]), (n2_turned, [(dcq, 0, columns)])],
            [(mem_turned, [(dck, 0, columns), (dcv, 0, columns)])],
        ]),
        pair_orders, peers,
    )
    mem_packed, mem_token = call(
        pack_sum_body, [shape((slots, width), BF16), Far(shape((8, 128), F32))], [taken, d_mem, pack2_there],
        after=[cross_sum.halves[0]],
        weight=LIGHT,
    )
    mem_back = exchange_rows(mem_packed, peers)
    ff_token = ff_sum.step(after=[mem_token])
    g1_own, g1_turned, dsq, dsk, dsv, dn1, dn1_sent, dgain2, diag = call(
        self_back_body,
        [Far(half32), turned, narrow, narrow, narrow, Far(half32), half16, Far(gain_shape),
         Far(shape((heads, 8, 3 * MAX_DIST), F32))],
        [
            core_ref, Far(pack2), pack2_there, h1_far, g2, gain_two, self_out, Far(sv),
            Far(self_probs), Far(sk), Far(sq), Far(self_qkv),
        ],
        flops=8 * square + 14 * scores * HEAD_DIM,
        scratch=[
            pltpu.VMEM((rows, columns), BF16), pltpu.VMEM((rows, width), F32),
            pltpu.VMEM((rows, width), BF16),
        ],
        smem=(0,),
        after=[ff_token],
    )

    def unpack(values, line):
        return call(unpack_body, [Far(half16)], [line, values], weight=LIGHT)[0]

    dn1_there = swap(dn1_sent)
    self_sides = [
        [(g1_turned, [(Far(self_mix), 0, columns)]), (Far(n1_turned), [(dsq, 0, columns)])],
        [(Far(n1_turned), [(dsk, 0, columns), (dsv, 0, columns)])],
    ]
    merged = bits == 4
    if merged:
        ca, _, cb, _ = cross_sum.halves
        keep_sa, send_x, keep_sb, send_y, keep_ca, keep_cb = weight_halves(
            me_ref, peers, pair_orders, self_sides, weight=AFTER_SELF, after=[dgain2],
            also=[ca, cross_sum.arrived[0], cb, cross_sum.arrived[1]],
        )
        from_x, from_y = neighbour(send_x, 0, peers), neighbour(send_y, 1, peers)
        self_token = keep_sa
    else:
        self_sum = Sum(
            weight_halves(
                me_ref, peers, pair_orders, self_sides, weight=AFTER_SELF, after=[dgain2]
            ),
            pair_orders, peers,
        )
        self_token = self_sum.halves[0]
    ff_token = self_token
    if FF_FIRST:
        ff_token = ff_sum.step(after=[self_token])
    [packed] = call(
        partial(last_body, peers),
        [shape((slots + peers * EXTRA, width), BF16)],
        [
            core_ref, taken_wide, dn1_there, Far(dn1), Far(x), gain_one, Far(g1_own), dgain2, dgain3,
            diag, jnp.asarray(bucket_hot, F32),
        ],
        smem=(0,),
        after=[ff_token, Near(mem_back)],
        weight=LIGHT,
    )
    back = exchange_rows(packed, peers)
    token = Near(packed)
    half = width // 8
    if merged:
        if not FF_FIRST:
            token = ff_sum.step(after=[token])
        wide_pair = columns * 4

        def two():
            keep_sa2, keep_sb2, send_x2, send_y2, keep_c, send_z = call(
                add_both_body,
                [Far(shape((2 * half, 2 * columns), BF16))] * 2
                + [shape((2 * half, 2 * columns), BF16)] * 2
                + [Far(shape((half, wide_pair), BF16)), shape((half, wide_pair), BF16)],
                [keep_sa, keep_sb, keep_ca, keep_cb, from_x, from_y],
                after=[token],
                weight=LIGHT,
            )
            return keep_sa2, keep_sb2, keep_c, (
                neighbour(send_x2, 0, peers), neighbour(send_y2, 1, peers), neighbour(send_z, 2, peers)
            )

        if TWO_FIRST:
            keep_sa2, keep_sb2, keep_c, arrived_two = two()
            token = ff_sum.step(after=[keep_sa2])
        else:
            token = ff_sum.step(after=[token])
            keep_sa2, keep_sb2, keep_c, arrived_two = two()
            token = keep_sa2
        keep_s, send_z, keep_c, send_w = call(
            add_last_body,
            pieces(half, wide_pair) + pieces(half // 2, wide_pair),
            [keep_sa2, keep_sb2, keep_c, *arrived_two],
            after=[token],
            weight=LIGHT,
        )
        cross_arrived, from_z = neighbour(send_w, 3, peers), neighbour(send_z, 2, peers)
        keep_s, send_w = call(
            add_split_body, pieces(half // 2, wide_pair), [keep_s, from_z], weight=LIGHT
        )
        self_arrived = neighbour(send_w, 3, peers)
        cross_pair, self_pair = [keep_c, cross_arrived], [keep_s, self_arrived]
    else:
        for group in (cross_sum, ff_sum, self_sum, cross_sum, ff_sum, self_sum):
            token = group.step(after=[token])
        for group in (cross_sum, self_sum):
            while group.place < bits:
                group.step()
        cross_pair, self_pair = cross_sum.pairs(), self_sum.pairs()
    ff_in_total, ff_out_total = ff_sum.finish(
        [shape((block, units), F32), shape((block, units), F32)],
        ((0, None, [(units, 2 * units)]), (1, None, [(0, units)])),
        weight=LAST_WEIGHT,
    )
    memory_grad = unpack(mem_back, sent)
    input_grad, small = call(
        partial(unpack_last_body, peers),
        [Far(half16), shape((8, width), F32)],
        [sent_wide, back],
        after=[ff_in_total, memory_grad],
        weight=LIGHT,
    )
    moves = ((0, None, [(0, columns)]),) + tuple(
        (1, i, [((i + 1) * columns, (i + 2) * columns)]) for i in range(3)
    )

    def finish(pair, after):
        outs = [Far(shape((block, columns), F32)), Far(shape((3, block, columns), F32))]
        return call(partial(finish_body, moves), outs, pair, after=after, weight=LIGHT)

    cross_out_total, cross_qkv_total = finish(cross_pair, [input_grad])
    self_out_total, self_qkv_total = finish(self_pair, [cross_out_total])
    small = small + swap(small)
    gains_total = small[:3]
    bias_total = small[3, : 2 * heads * buckets].reshape(heads, 2, buckets).transpose(2, 1, 0)
    bias_total = bias_total.reshape(buckets, 2 * heads)
    return (
        block_out,
        input_grad,
        memory_grad,
        gains_total,
        bias_total,
        self_qkv_total,
        self_out_total.T,
        cross_qkv_total,
        cross_out_total.T,
        ff_in_total,
        ff_out_total.T,
    )


def solution(mesh):
    both = ("dp", "mp")
    in_specs = (
        P(both, None),
        P(both, None),
        P(both, None),
        P("dp", None),
        P(),
        P(),
        P(None, None, "mp"),
        P("mp", None),
        P(None, None, "mp"),
        P("mp", None),
        P(None, "mp"),
        P("mp", None),
        P(None, "mp"),
    )
    out_specs = (
        P(both, None),
        P(both, None),
        P(both, None),
        P(),
        P(),
        P(None, "dp", "mp"),
        P("mp", "dp"),
        P(None, "dp", "mp"),
        P("mp", "dp"),
        P("dp", "mp"),
        P("mp", "dp"),
    )
    return jax.shard_map(local, mesh=mesh, in_specs=in_specs, out_specs=out_specs, check_vma=False)
```

profile of v0, /device:TPU:0, one launch (start us, length us, event | category | flops | bytes accessed | tf_op | source)
XLA Modules:
  0.0 232.8 jit_solution(15937263158244710599)
XLA Ops:
  1.9 3.7 %shard_map.230 = (bf16[512,1536]{1,0:T(8,128)(2,1)}, s32[1,512]{1,0:T(1,128)}) custom-call(s32[16,16]{1,0:T(8,128)S(1)} %copy-done.46, s32[1]{0:T(128)} %bitcast.1.refs_1_.refs_0_, bf16[256,768]{1,0:T(8,128)(2,1)} %refs_2_.1, bf16[256,768]{1,0:T(8,128)(2,1)} %refs_3_.3), custom_call_target="tpu_custom_call" | custom-call | flops 30000001024 | tf_op jit(solution)/shard_map/pallas_call | solution.py:190
  5.6 8.0 %all-to-all-start = ((bf16[16,32,1536]{2,1,0:T(8,128)(2,1)}), bf16[16,32,1536]{2,1,0:T(8,128)(2,1)S(1)}, u32[]{:S(2)}, u32[]{:S(2)}) async-start(bf16[16,32,1536]{2,1,0:T(8,128)(2,1)} %bitcast.3), calls=%async_computation | async-start | bytes 3145728 | tf_op jit(solution)/shard_map/all_to_all | solution.py:757
  13.8 2.6 %shard_map.231 = (bf16[6,256,512]{2,1,0:T(8,128)(2,1)}, f32[512,512]{1,0:T(8,128)}, s32[1,512]{1,0:T(1,128)}, s32[1,640]{1,0:T(1,128)}, s32[1,640]{1,0:T(1,128)}) custom-call(s32[16,16]{1,0:T(8,128)S(1)} %copy-done.47, s32[1]{0:T(128)} %bitcast.1.refs_1_.refs_0_, f32[6,256]{1,0:T(8,128)S(1)} %convolution_bitcast_fusion.refs_2_, s32[1,512]{1,0:T(1,128)S(1)} %copy-done.48, ...), custom_call_target="tpu_custom_call" | custom-call | flops 30000001024 | tf_op jit(solution)/shard_map/pallas_call | solution.py:190
  17.7 30.2 %all-to-all-done = bf16[16,32,1536]{2,1,0:T(8,128)(2,1)S(1)} async-done(((bf16[16,32,1536]{2,1,0:T(8,128)(2,1)}), bf16[16,32,1536]{2,1,0:T(8,128)(2,1)S(1)}, u32[]{:S(2)}, u32[]{:S(2)}) %all-to-all-start) | async-done | bytes 1572896 | tf_op jit(solution)/shard_map/all_to_all | solution.py:757
  48.7 2.2 collective-permute-done.1.refs_2_
  50.9 7.2 %shard_map.234 = (bf16[512,768]{1,0:T(8,128)(2,1)}, bf16[768,512]{1,0:T(8,128)(2,1)}, bf16[512,384]{1,0:T(8,128)(2,1)}, bf16[512,384]{1,0:T(8,128)(2,1)}, bf16[5...) custom-call(s32[1]{0:T(128)} %bitcast.refs_0_, ...), custom_call_target="tpu_custom_call" | custom-call | flops 30000001024 | tf_op jit(solution)/shard_map/pallas_call | solution.py:190
  58.3 1.8 shard_map.235
  60.5 8.5 %shard_map.236 = (f32[512,768]{1,0:T(8,128)S(1)}, f32[512,768]{1,0:T(8,128)}, bf16[768,512]{1,0:T(8,128)(2,1)}, bf16[512,384]{1,0:T(8,128)(2,1)}, bf16[6,512,512...) custom-call(bf16[512,768]{1,0:T(8,128)(2,1)S(1)} %get-tuple-element.120.refs_0_, ...), custom_call_target="tpu_custom_call" | custom-call | flops 30000001024 | tf_op jit(solution)/shard_map/pallas_call | solution.py:190
  69.2 2.1 collective-permute-done.3.refs_2_
  71.4 6.8 %shard_map.237 = (bf16[768,512]{1,0:T(8,128)(2,1)S(1)}, f32[512,768]{1,0:T(8,128)S(1)}, bf16[512,1536]{1,0:T(8,128)(2,1)S(1)}, bf16[512,1536]{1,0:T(8,128)(2,1)S...) custom-call(s32[1]{0:T(128)} %bitcast.refs_0_, bf16[512,768]{1,0:T(8,128)(2,1)S(1)} %get-tuple-element.124.refs_1_, ...), custom_call_target="tpu_custom_call" | custom-call | flops 30000001024 | tf_op jit(solution)/shard_map/pallas_call | solution.py:190
  78.4 6.5 %shard_map.238 = (bf16[384,1024]{1,0:T(8,128)(2,1)}, bf16[384,1024]{1,0:T(8,128)(2,1)}, bf16[384,1024]{1,0:T(8,128)(2,1)}, bf16[384,1024]{1,0:T(8,128)(2,1)}, bf...) custom-call(s32[1]{0:T(128)} %bitcast.1.refs_1_.refs_0_, bf16[768,512]{1,0:T(8,128)(2,1)} %get-tuple-element.118.refs_3_.refs_1_, ...), custom_call_target="tpu_custom_call" | custom-call | flops 30000001024 | tf_op jit(solution)/shard_map/pallas_call | solution.py:190
  86.2 2.7 %collective-permute-start.7 = (bf16[384,1024]{1,0:T(8,128)(2,1)}, bf16[384,1024]{1,0:T(8,128)(2,1)}, u32[]{:S(2)}, u32[]{:S(2)}) collective-permute-start(bf16[384,1024]{1,0:T(8,128)(2,1)} %get-tuple-element.148), channel_id=1, source_target_pairs={{0,4},{2,6},{4,0},{6,2},{8,12},{10,14},{12,8},{14,10},{16,20},{18,... | collective-permute-start | bytes 2359304 | tf_op jit(solution)/shard_map/ppermute | solution.py:765
  88.8 4.0 %collective-permute-start.8 = (bf16[384,1024]{1,0:T(8,128)(2,1)}, bf16[384,1024]{1,0:T(8,128)(2,1)}, u32[]{:S(2)}, u32[]{:S(2)}) collective-permute-start(bf16[384,1024]{1,0:T(8,128)(2,1)} %get-tuple-element.150), channel_id=1, source_target_pairs={{0,8},{2,10},{4,12},{6,14},{8,0},{10,2},{12,4},{14,6},{16,24},{18,... | collective-permute-start | bytes 2359304 | tf_op jit(solution)/shard_map/ppermute | solution.py:765
  92.9 20.5 %shard_map.239 = (f32[512,768]{1,0:T(8,128)}, bf16[768,512]{1,0:T(8,128)(2,1)S(1)}, bf16[512,384]{1,0:T(8,128)(2,1)S(1)}, bf16[512,384]{1,0:T(8,128)(2,1)S(1)}, ...) custom-call(s32[1]{0:T(128)} %bitcast.refs_0_, ...), custom_call_target="tpu_custom_call" | custom-call | flops 30000001024 | tf_op jit(solution)/shard_map/pallas_call | solution.py:190
  113.5 3.7 %shard_map.240 = (bf16[384,768]{1,0:T(8,128)(2,1)}, bf16[384,768]{1,0:T(8,128)(2,1)}, bf16[384,768]{1,0:T(8,128)(2,1)}, bf16[384,768]{1,0:T(8,128)(2,1)}) custom-call(s32[1]{0:T(128)} %bitcast.1.refs_1_.refs_0_, bf16[768,512]{1,0:T(8,128)(2,1)S(1)} %get-tuple-element.152.refs_1_, bf16[512,384]{1,0:T(8,128)(2,1)S(1)} %copy-done.59, ...), custom_call_target="tpu_custom_call" | custom-call | flops 30000001024 | tf_op jit(solution)/shard_map/pallas_call | solution.py:190
  118.2 1.6 shard_map.241
  119.8 4.6 %all-to-all-start.1 = ((bf16[16,32,768]{2,1,0:T(8,128)(2,1)}), bf16[16,32,768]{2,1,0:T(8,128)(2,1)S(1)}, u32[]{:S(2)}, u32[]{:S(2)}) async-start(bf16[16,32,768]{2,1,0:T(8,128)(2,1)} %bitcast.5), calls=%async_computation.1 | async-start | bytes 1572864 | tf_op jit(solution)/shard_map/all_to_all | solution.py:757
  125.6 3.2 %shard_map.242 = (bf16[192,1024]{1,0:T(8,128)(2,1)}, bf16[192,1024]{1,0:T(8,128)(2,1)S(1)}, bf16[192,1024]{1,0:T(8,128)(2,1)}, bf16[192,1024]{1,0:T(8,128)(2,1)S...) custom-call(bf16[384,1024]{1,0:T(8,128)(2,1)S(1)} %copy-done.5, ...), custom_call_target="tpu_custom_call" | custom-call | flops 1000000 | tf_op jit(solution)/shard_map/pallas_call | solution.py:190
  128.8 2.0 collective-permute-start.10
  133.7 11.9 %shard_map.243 = (f32[256,768]{1,0:T(8,128)}, bf16[768,512]{1,0:T(8,128)(2,1)S(1)}, bf16[512,384]{1,0:T(8,128)(2,1)S(1)}, bf16[512,384]{1,0:T(8,128)(2,1)S(1)}, ...) custom-call(s32[1]{0:T(128)} %bitcast.refs_0_, ...), custom_call_target="tpu_custom_call" | custom-call | flops 30000001024 | tf_op jit(solution)/shard_map/pallas_call | solution.py:190
  145.8 6.9 %shard_map.244 = (bf16[384,768]{1,0:T(8,128)(2,1)}, bf16[576,768]{1,0:T(8,128)(2,1)}, bf16[384,768]{1,0:T(8,128)(2,1)}, bf16[576,768]{1,0:T(8,128)(2,1)}, bf16[1...) custom-call(s32[1]{0:T(128)} %bitcast.1.refs_1_.refs_0_, bf16[768,512]{1,0:T(8,128)(2,1)S(1)} %get-tuple-element.173.refs_1_, ...), custom_call_target="tpu_custom_call" | custom-call | flops 3000000000 | tf_op jit(solution)/shard_map/pallas_call | solution.py:190
  157.0 4.0 %shard_map.246.refs_6_ = bf16[640,768]{1,0:T(8,128)(2,1)} custom-call(s32[1]{0:T(128)} %bitcast.refs_0_, s32[1,640]{1,0:T(1,128)S(1)} %copy-done.30, bf16[256,768]{1,0:T(8,128)(2,1)S(1)} %collective-permute-done.9.refs_2_, f32[256,768]{1,0:T(8,128)} %get-tuple-element.163.refs_3_, bf16[512,768]{1,0:T(8,128)(2,1)} %get-tuple-element.121.refs_4_.refs_2_, ...), custom_call_target="tpu_custom_call" | custom-call | flops 1000000 | tf_op jit(solution)/shard_map/pallas_call | solution.py:190
  161.0 5.9 %all-to-all-start.2 = ((bf16[16,40,768]{2,1,0:T(8,128)(2,1)}), bf16[16,40,768]{2,1,0:T(8,128)(2,1)S(1)}, u32[]{:S(2)}, u32[]{:S(2)}) async-start(bf16[16,40,768]{2,1,0:T(8,128)(2,1)} %bitcast.7), calls=%async_computation.2 | async-start | bytes 1966080 | tf_op jit(solution)/shard_map/all_to_all | solution.py:757
  166.9 1.9 collective-permute-start.15
  168.8 6.9 %collective-permute-done.18.refs_4_ = bf16[576,768]{1,0:T(8,128)(2,1)S(1)} collective-permute-done((bf16[576,768]{1,0:T(8,128)(2,1)}, bf16[576,768]{1,0:T(8,128)(2,1)S(1)}, u32[]{:S(2)}, u32[]{:S(2)}) %collective-permute-start.18) | collective-permute-done | bytes 884768 | tf_op jit(solution)/shard_map/ppermute | solution.py:765
  175.8 7.0 %collective-permute-done.19.refs_5_ = bf16[576,768]{1,0:T(8,128)(2,1)} collective-permute-done((bf16[576,768]{1,0:T(8,128)(2,1)}, bf16[576,768]{1,0:T(8,128)(2,1)}, u32[]{:S(2)}, u32[]{:S(2)}) %collective-permute-start.19) | collective-permute-done | bytes 884768 | tf_op jit(solution)/shard_map/ppermute | solution.py:765
  184.8 2.3 shard_map.247
  187.1 1.5 collective-permute-start.22
  191.2 8.9 %collective-permute-done.16.refs_3_ = bf16[96,1024]{1,0:T(8,128)(2,1)S(1)} collective-permute-done((bf16[96,1024]{1,0:T(8,128)(2,1)S(1)}, bf16[96,1024]{1,0:T(8,128)(2,1)S(1)}, u32[]{:S(2)}, u32[]{:S(2)}) %collective-permute-start.16) | collective-permute-done | bytes 196640 | tf_op jit(solution)/shard_map/ppermute | solution.py:765
  202.2 3.4 %collective-permute-start.20 = (bf16[48,3072]{1,0:T(8,128)(2,1)S(1)}, bf16[48,3072]{1,0:T(8,128)(2,1)S(1)}, u32[]{:S(2)}, u32[]{:S(2)}) collective-permute-start(bf16[48,3072]{1,0:T(8,128)(2,1)S(1)} %get-tuple-element.197), channel_id=1, source_target_pairs={{0,16},{2,18},{4,20},{6,22},{8,24},{10,26},{12,28},{14,30},{16,0},... | collective-permute-start | bytes 884744 | tf_op jit(solution)/shard_map/ppermute | solution.py:765
  206.9 9.1 %collective-permute-done.25.refs_1_ = bf16[96,1536]{1,0:T(8,128)(2,1)S(1)} collective-permute-done((bf16[96,1536]{1,0:T(8,128)(2,1)S(1)}, bf16[96,1536]{1,0:T(8,128)(2,1)S(1)}, u32[]{:S(2)}, u32[]{:S(2)}) %collective-permute-start.25) | collective-permute-done | bytes 294944 | tf_op jit(solution)/shard_map/ppermute | solution.py:765
  217.7 8.4 %collective-permute-done.20.refs_1_ = bf16[48,3072]{1,0:T(8,128)(2,1)S(1)} collective-permute-done((bf16[48,3072]{1,0:T(8,128)(2,1)S(1)}, bf16[48,3072]{1,0:T(8,128)(2,1)S(1)}, u32[]{:S(2)}, u32[]{:S(2)}) %collective-permute-start.20) | collective-permute-done | bytes 294944 | tf_op jit(solution)/shard_map/ppermute | solution.py:765
  (188 shorter events, 30.8 us)
Async XLA Ops:
  0.7 15.8 %collective-permute-start = (bf16[256,768]{1,0:T(8,128)(2,1)}, bf16[256,768]{1,0:T(8,128)(2,1)S(1)}, u32[]{:S(2)}, u32[]{:S(2)}) collective-permute-start(bf16[256,768]{1,0:T(8,128)(2,1)} %refs_1_.1), channel_id=1, source_target_pairs={{0,1},{1,0},{2,3},{3,2},{4,5},{5,4},{6,7},{7,6},{8,9},{9,8},{10,11... | collective-permute-start | bytes 1179656 | tf_op jit(solution)/shard_map/ppermute | solution.py:761
  5.6 42.3 %all-to-all-start = ((bf16[16,32,1536]{2,1,0:T(8,128)(2,1)}), bf16[16,32,1536]{2,1,0:T(8,128)(2,1)S(1)}, u32[]{:S(2)}, u32[]{:S(2)}) async-start(bf16[16,32,1536]{2,1,0:T(8,128)(2,1)} %bitcast.3), calls=%async_computation | async-start | bytes 3145728 | tf_op jit(solution)/shard_map/all_to_all | solution.py:757
  16.4 31.5 %copy-start.32 = (s32[1,512]{1,0:T(1,128)S(1)}, s32[1,512]{1,0:T(1,128)}, u32[]{:S(2)}) copy-start(s32[1,512]{1,0:T(1,128)} %get-tuple-element.115.refs_0_) | copy-start | bytes 6148
  48.5 2.4 %collective-permute-start.1 = (bf16[256,1536]{1,0:T(8,128)(2,1)S(1)}, bf16[256,1536]{1,0:T(8,128)(2,1)S(1)}, u32[]{:S(2)}, u32[]{:S(2)}) collective-permute-start(bf16[256,1536]{1,0:T(8,128)(2,1)S(1)} %shard_map.233.refs_1_), channel_id=1, source_target_pairs={{0,1},{1,0},{2,3},{3,2},{4,5},{5,4},{6,7},{7,6},{8,9},{9,8},{10,11... | collective-permute-start | bytes 2359304 | tf_op jit(solution)/shard_map/ppermute | solution.py:761
  58.1 2.4 %collective-permute-start.2 = (bf16[512,768]{1,0:T(8,128)(2,1)S(1)}, bf16[512,768]{1,0:T(8,128)(2,1)S(1)}, u32[]{:S(2)}, u32[]{:S(2)}) collective-permute-start(bf16[512,768]{1,0:T(8,128)(2,1)S(1)} %get-tuple-element.120.refs_0_), channel_id=1, source_target_pairs={{0,1},{1,0},{2,3},{3,2},{4,5},{5,4},{6,7},{7,6},{8,9},{9,8},{10,11... | collective-permute-start | bytes 2359304 | tf_op jit(solution)/shard_map/ppermute | solution.py:761
  69.0 2.4 %collective-permute-start.3 = (bf16[512,768]{1,0:T(8,128)(2,1)S(1)}, bf16[512,768]{1,0:T(8,128)(2,1)S(1)}, u32[]{:S(2)}, u32[]{:S(2)}) collective-permute-start(bf16[512,768]{1,0:T(8,128)(2,1)S(1)} %get-tuple-element.124.refs_1_), channel_id=1, source_target_pairs={{0,1},{1,0},{2,3},{3,2},{4,5},{5,4},{6,7},{7,6},{8,9},{9,8},{10,11... | collective-permute-start | bytes 2359304 | tf_op jit(solution)/shard_map/ppermute | solution.py:761
  78.2 14.7 %collective-permute-start.4 = (bf16[768,768]{1,0:T(8,128)(2,1)S(1)}, bf16[768,768]{1,0:T(8,128)(2,1)S(1)}, u32[]{:S(2)}, u32[]{:S(2)}) collective-permute-start(bf16[768,768]{1,0:T(8,128)(2,1)S(1)} %get-tuple-element.127.refs_1_), channel_id=1, source_target_pairs={{0,1},{1,0},{2,3},{3,2},{4,5},{5,4},{6,7},{7,6},{8,9},{9,8},{10,11... | collective-permute-start | bytes 3538952 | tf_op jit(solution)/shard_map/ppermute | solution.py:761
  84.9 39.5 %collective-permute-start.6 = (bf16[384,1024]{1,0:T(8,128)(2,1)}, bf16[384,1024]{1,0:T(8,128)(2,1)}, u32[]{:S(2)}, u32[]{:S(2)}) collective-permute-start(bf16[384,1024]{1,0:T(8,128)(2,1)} %get-tuple-element.146), channel_id=1, source_target_pairs={{0,2},{2,0},{4,6},{6,4},{8,10},{10,8},{12,14},{14,12},{16,18},{18,... | collective-permute-start | bytes 2359304 | tf_op jit(solution)/shard_map/ppermute | solution.py:765
  86.2 38.3 %collective-permute-start.7 = (bf16[384,1024]{1,0:T(8,128)(2,1)}, bf16[384,1024]{1,0:T(8,128)(2,1)}, u32[]{:S(2)}, u32[]{:S(2)}) collective-permute-start(bf16[384,1024]{1,0:T(8,128)(2,1)} %get-tuple-element.148), channel_id=1, source_target_pairs={{0,4},{2,6},{4,0},{6,2},{8,12},{10,14},{12,8},{14,10},{16,20},{18,... | collective-permute-start | bytes 2359304 | tf_op jit(solution)/shard_map/ppermute | solution.py:765
  88.8 35.6 %collective-permute-start.8 = (bf16[384,1024]{1,0:T(8,128)(2,1)}, bf16[384,1024]{1,0:T(8,128)(2,1)}, u32[]{:S(2)}, u32[]{:S(2)}) collective-permute-start(bf16[384,1024]{1,0:T(8,128)(2,1)} %get-tuple-element.150), channel_id=1, source_target_pairs={{0,8},{2,10},{4,12},{6,14},{8,0},{10,2},{12,4},{14,6},{16,24},{18,... | collective-permute-start | bytes 2359304 | tf_op jit(solution)/shard_map/ppermute | solution.py:765
  113.4 4.7 %collective-permute-start.5 = (bf16[768,768]{1,0:T(8,128)(2,1)}, bf16[768,768]{1,0:T(8,128)(2,1)S(1)}, u32[]{:S(2)}, u32[]{:S(2)}) collective-permute-start(bf16[768,768]{1,0:T(8,128)(2,1)} %get-tuple-element.139.refs_1_), channel_id=1, source_target_pairs={{0,1},{1,0},{2,3},{3,2},{4,5},{5,4},{6,7},{7,6},{8,9},{9,8},{10,11... | collective-permute-start | bytes 3538952 | tf_op jit(solution)/shard_map/ppermute | solution.py:761
  117.2 28.5 %collective-permute-start.13 = (bf16[384,768]{1,0:T(8,128)(2,1)}, bf16[384,768]{1,0:T(8,128)(2,1)}, u32[]{:S(2)}, u32[]{:S(2)}) collective-permute-start(bf16[384,768]{1,0:T(8,128)(2,1)} %get-tuple-element.179), channel_id=1, source_target_pairs={{0,2},{2,0},{4,6},{6,4},{8,10},{10,8},{12,14},{14,12},{16,18},{18,... | collective-permute-start | bytes 1769480 | tf_op jit(solution)/shard_map/ppermute | solution.py:765
  118.1 27.7 %collective-permute-start.14 = (bf16[384,768]{1,0:T(8,128)(2,1)}, bf16[384,768]{1,0:T(8,128)(2,1)}, u32[]{:S(2)}, u32[]{:S(2)}) collective-permute-start(bf16[384,768]{1,0:T(8,128)(2,1)} %get-tuple-element.181), channel_id=1, source_target_pairs={{0,4},{2,6},{4,0},{6,2},{8,12},{10,14},{12,8},{14,10},{16,20},{18,... | collective-permute-start | bytes 1769480 | tf_op jit(solution)/shard_map/ppermute | solution.py:765
  119.8 37.2 %all-to-all-start.1 = ((bf16[16,32,768]{2,1,0:T(8,128)(2,1)}), bf16[16,32,768]{2,1,0:T(8,128)(2,1)S(1)}, u32[]{:S(2)}, u32[]{:S(2)}) async-start(bf16[16,32,768]{2,1,0:T(8,128)(2,1)} %bitcast.5), calls=%async_computation.1 | async-start | bytes 1572864 | tf_op jit(solution)/shard_map/all_to_all | solution.py:757
  128.8 24.6 %collective-permute-start.10 = (bf16[192,1024]{1,0:T(8,128)(2,1)S(1)}, bf16[192,1024]{1,0:T(8,128)(2,1)S(1)}, u32[]{:S(2)}, u32[]{:S(2)}) collective-permute-start(bf16[192,1024]{1,0:T(8,128)(2,1)S(1)} %get-tuple-element.168), channel_id=1, source_target_pairs={{0,4},{2,6},{4,0},{6,2},{8,12},{10,14},{12,8},{14,10},{16,20},{18,... | collective-permute-start | bytes 1179656 | tf_op jit(solution)/shard_map/ppermute | solution.py:765
  130.8 23.2 %collective-permute-start.11 = (bf16[192,1024]{1,0:T(8,128)(2,1)S(1)}, bf16[192,1024]{1,0:T(8,128)(2,1)S(1)}, u32[]{:S(2)}, u32[]{:S(2)}) collective-permute-start(bf16[192,1024]{1,0:T(8,128)(2,1)S(1)} %get-tuple-element.170), channel_id=1, source_target_pairs={{0,8},{2,10},{4,12},{6,14},{8,0},{10,2},{12,4},{14,6},{16,24},{18,... | collective-permute-start | bytes 1179656 | tf_op jit(solution)/shard_map/ppermute | solution.py:765
  132.3 21.7 %collective-permute-start.12 = (bf16[192,1024]{1,0:T(8,128)(2,1)S(1)}, bf16[192,1024]{1,0:T(8,128)(2,1)S(1)}, u32[]{:S(2)}, u32[]{:S(2)}) collective-permute-start(bf16[192,1024]{1,0:T(8,128)(2,1)S(1)} %get-tuple-element.172), channel_id=1, source_target_pairs={{0,2},{2,0},{4,6},{6,4},{8,10},{10,8},{12,14},{14,12},{16,18},{18,... | collective-permute-start | bytes 1179656 | tf_op jit(solution)/shard_map/ppermute | solution.py:765
  145.7 11.3 %collective-permute-start.9 = (bf16[256,768]{1,0:T(8,128)(2,1)S(1)}, bf16[256,768]{1,0:T(8,128)(2,1)S(1)}, u32[]{:S(2)}, u32[]{:S(2)}) collective-permute-start(bf16[256,768]{1,0:T(8,128)(2,1)S(1)} %get-tuple-element.162), channel_id=1, source_target_pairs={{0,1},{1,0},{2,3},{3,2},{4,5},{5,4},{6,7},{7,6},{8,9},{9,8},{10,11... | collective-permute-start | bytes 1179656 | tf_op jit(solution)/shard_map/ppermute | solution.py:761
  152.8 23.0 %collective-permute-start.18 = (bf16[576,768]{1,0:T(8,128)(2,1)}, bf16[576,768]{1,0:T(8,128)(2,1)S(1)}, u32[]{:S(2)}, u32[]{:S(2)}) collective-permute-start(bf16[576,768]{1,0:T(8,128)(2,1)} %get-tuple-element.193), channel_id=1, source_target_pairs={{0,2},{2,0},{4,6},{6,4},{8,10},{10,8},{12,14},{14,12},{16,18},{18,... | collective-permute-start | bytes 2654216 | tf_op jit(solution)/shard_map/ppermute | solution.py:765
  153.4 29.3 %collective-permute-start.19 = (bf16[576,768]{1,0:T(8,128)(2,1)}, bf16[576,768]{1,0:T(8,128)(2,1)}, u32[]{:S(2)}, u32[]{:S(2)}) collective-permute-start(bf16[576,768]{1,0:T(8,128)(2,1)} %get-tuple-element.194), channel_id=1, source_target_pairs={{0,4},{2,6},{4,0},{6,2},{8,12},{10,14},{12,8},{14,10},{16,20},{18,... | collective-permute-start | bytes 2654216 | tf_op jit(solution)/shard_map/ppermute | solution.py:765
  161.0 66.1 %all-to-all-start.2 = ((bf16[16,40,768]{2,1,0:T(8,128)(2,1)}), bf16[16,40,768]{2,1,0:T(8,128)(2,1)S(1)}, u32[]{:S(2)}, u32[]{:S(2)}) async-start(bf16[16,40,768]{2,1,0:T(8,128)(2,1)} %bitcast.7), calls=%async_computation.2 | async-start | bytes 1966080 | tf_op jit(solution)/shard_map/all_to_all | solution.py:757
  166.9 22.8 %collective-permute-start.15 = (bf16[96,1024]{1,0:T(8,128)(2,1)}, bf16[96,1024]{1,0:T(8,128)(2,1)S(1)}, u32[]{:S(2)}, u32[]{:S(2)}) collective-permute-start(bf16[96,1024]{1,0:T(8,128)(2,1)} %copy-done.45), channel_id=1, source_target_pairs={{0,8},{2,10},{4,12},{6,14},{8,0},{10,2},{12,4},{14,6},{16,24},{18,... | collective-permute-start | bytes 589832 | tf_op jit(solution)/shard_map/ppermute | solution.py:765
  187.1 14.1 %collective-permute-start.22 = (bf16[192,768]{1,0:T(8,128)(2,1)S(1)}, bf16[192,768]{1,0:T(8,128)(2,1)S(1)}, u32[]{:S(2)}, u32[]{:S(2)}) collective-permute-start(bf16[192,768]{1,0:T(8,128)(2,1)S(1)} %get-tuple-element.203), channel_id=1, source_target_pairs={{0,2},{2,0},{4,6},{6,4},{8,10},{10,8},{12,14},{14,12},{16,18},{18,... | collective-permute-start | bytes 884744 | tf_op jit(solution)/shard_map/ppermute | solution.py:765
  188.6 12.6 %collective-permute-start.23 = (bf16[192,768]{1,0:T(8,128)(2,1)S(1)}, bf16[192,768]{1,0:T(8,128)(2,1)S(1)}, u32[]{:S(2)}, u32[]{:S(2)}) collective-permute-start(bf16[192,768]{1,0:T(8,128)(2,1)S(1)} %get-tuple-element.204), channel_id=1, source_target_pairs={{0,4},{2,6},{4,0},{6,2},{8,12},{10,14},{12,8},{14,10},{16,20},{18,... | collective-permute-start | bytes 884744 | tf_op jit(solution)/shard_map/ppermute | solution.py:765
  189.7 11.6 %collective-permute-start.24 = (bf16[96,1536]{1,0:T(8,128)(2,1)S(1)}, bf16[96,1536]{1,0:T(8,128)(2,1)S(1)}, u32[]{:S(2)}, u32[]{:S(2)}) collective-permute-start(bf16[96,1536]{1,0:T(8,128)(2,1)S(1)} %get-tuple-element.205), channel_id=1, source_target_pairs={{0,8},{2,10},{4,12},{6,14},{8,0},{10,2},{12,4},{14,6},{16,24},{18,... | collective-permute-start | bytes 884744 | tf_op jit(solution)/shard_map/ppermute | solution.py:765
  189.7 10.5 %collective-permute-start.16 = (bf16[96,1024]{1,0:T(8,128)(2,1)S(1)}, bf16[96,1024]{1,0:T(8,128)(2,1)S(1)}, u32[]{:S(2)}, u32[]{:S(2)}) collective-permute-start(bf16[96,1024]{1,0:T(8,128)(2,1)S(1)} %copy-done.44), channel_id=1, source_target_pairs={{0,2},{2,0},{4,6},{6,4},{8,10},{10,8},{12,14},{14,12},{16,18},{18,... | collective-permute-start | bytes 589832 | tf_op jit(solution)/shard_map/ppermute | solution.py:765
  189.8 10.6 %collective-permute-start.17 = (bf16[96,1024]{1,0:T(8,128)(2,1)S(1)}, bf16[96,1024]{1,0:T(8,128)(2,1)S(1)}, u32[]{:S(2)}, u32[]{:S(2)}) collective-permute-start(bf16[96,1024]{1,0:T(8,128)(2,1)S(1)} %copy-done.42), channel_id=1, source_target_pairs={{0,4},{2,6},{4,0},{6,2},{8,12},{10,14},{12,8},{14,10},{16,20},{18,... | collective-permute-start | bytes 589832 | tf_op jit(solution)/shard_map/ppermute | solution.py:765
  202.1 13.9 %collective-permute-start.25 = (bf16[96,1536]{1,0:T(8,128)(2,1)S(1)}, bf16[96,1536]{1,0:T(8,128)(2,1)S(1)}, u32[]{:S(2)}, u32[]{:S(2)}) collective-permute-start(bf16[96,1536]{1,0:T(8,128)(2,1)S(1)} %get-tuple-element.207), channel_id=1, source_target_pairs={{0,8},{2,10},{4,12},{6,14},{8,0},{10,2},{12,4},{14,6},{16,24},{18,... | collective-permute-start | bytes 884744 | tf_op jit(solution)/shard_map/ppermute | solution.py:765
  202.2 24.0 %collective-permute-start.20 = (bf16[48,3072]{1,0:T(8,128)(2,1)S(1)}, bf16[48,3072]{1,0:T(8,128)(2,1)S(1)}, u32[]{:S(2)}, u32[]{:S(2)}) collective-permute-start(bf16[48,3072]{1,0:T(8,128)(2,1)S(1)} %get-tuple-element.197), channel_id=1, source_target_pairs={{0,16},{2,18},{4,20},{6,22},{8,24},{10,26},{12,28},{14,30},{16,0},... | collective-permute-start | bytes 884744 | tf_op jit(solution)/shard_map/ppermute | solution.py:765
  206.8 22.1 %collective-permute-start.27 = (bf16[48,1536]{1,0:T(8,128)(2,1)S(1)}, bf16[48,1536]{1,0:T(8,128)(2,1)S(1)}, u32[]{:S(2)}, u32[]{:S(2)}) collective-permute-start(bf16[48,1536]{1,0:T(8,128)(2,1)S(1)} %get-tuple-element.211), channel_id=1, source_target_pairs={{0,16},{2,18},{4,20},{6,22},{8,24},{10,26},{12,28},{14,30},{16,0},... | collective-permute-start | bytes 442376 | tf_op jit(solution)/shard_map/ppermute | solution.py:765
  217.7 12.8 %collective-permute-start.26 = (bf16[48,1536]{1,0:T(8,128)(2,1)S(1)}, bf16[48,1536]{1,0:T(8,128)(2,1)S(1)}, u32[]{:S(2)}, u32[]{:S(2)}) collective-permute-start(bf16[48,1536]{1,0:T(8,128)(2,1)S(1)} %get-tuple-element.209), channel_id=1, source_target_pairs={{0,16},{2,18},{4,20},{6,22},{8,24},{10,26},{12,28},{14,30},{16,0},... | collective-permute-start | bytes 442376 | tf_op jit(solution)/shard_map/ppermute | solution.py:765
  228.5 2.8 %collective-permute-start.21 = (f32[8,768]{1,0:T(8,128)S(1)}, f32[8,768]{1,0:T(8,128)S(1)}, u32[]{:S(2)}, u32[]{:S(2)}) collective-permute-start(f32[8,768]{1,0:T(8,128)S(1)} %get-tuple-element.200), channel_id=1, source_target_pairs={{0,1},{1,0},{2,3},{3,2},{4,5},{5,4},{6,7},{7,6},{8,9},{9,8},{10,11... | collective-permute-start | bytes 73736 | tf_op jit(solution)/shard_map/ppermute | solution.py:761
  (61 other events, 507.0 us)
where the time goes:
time: 237 us; the launch traced here: 233 us
  Pallas kernels  101 us (43%)
  waiting for transfers between devices  76.8 us (32%)
  starting transfers between devices  44.7 us (19%)
  local copies, waits for them, and re-layouts  8.43 us (4%)
    pallas_call x26, Pallas kernels, call(): pl.pallas_call(kernel, out_shape=[(pltpu.HBM if i in far_out else pltpu.V...  101 us
    ppermute x20, waiting for transfers between devices, neighbour(): return lax.ppermute(values, 'dp', [(i, i ^ 1 << bit) for i in range(peers)])  41.8 us
    all_to_all x3, waiting for transfers between devices, exchange_rows(): lax.all_to_all(blocks, 'dp', split_axis=0, concat_axis=0, tiled=True)  30.2 us
    ppermute x20, starting transfers between devices, neighbour(): return lax.ppermute(values, 'dp', [(i, i ^ 1 << bit) for i in range(peers)])  24.7 us
    all_to_all x3, starting transfers between devices, exchange_rows(): lax.all_to_all(blocks, 'dp', split_axis=0, concat_axis=0, tiled=True)  18.6 us
    unnamed x124, local copies, waits for them, and re-layouts  7.11 us
  transfers between devices with their start and end apart: 31, of which 12 were waited for; matrix products, arithmetic and copies ran while one was open for 0% of the time, Pallas kernels for 33%

commit v1 on v0

--- a/solution.py
+++ b/solution.py
@@ -20,8 +20,6 @@
 LIGHT = 10**6
 AFTER_SELF = 3 * 10**9
 LAST_WEIGHT = 7 * 10**9
-FF_FIRST = True
-TWO_FIRST = True
 FF_STEPS = 3
 EXTRA = 8
 
@@ -396,12 +394,13 @@
 
 def self_forward_body(
     core_ref, own_ref, other_ref, gain_ref, w_ref, mask_ref, bias_ref, wo_ref,
-    x_ref, nt_ref, q_ref, k_ref, v_ref, probs_ref, mix_ref, part_ref, n_ref,
+    x_ref, x_far_ref, nt_ref, q_ref, k_ref, v_ref, probs_ref, mix_ref, part_ref, n_ref,
 ):
     half, width = own_ref.shape[0], gain_ref.shape[1]
     x_ref[own_rows(core_ref, half), :] = own_ref[:, :width]
     x_ref[their_rows(core_ref, half), :] = other_ref[:, :width]
-    flush(x_ref)
+    x_far_ref[...] = x_ref[...]
+    flush(x_far_ref)
     x = x_ref[...].astype(F32)
     n_ref[...] = (x * rms_scale(x) * gain_ref[...]).astype(BF16)
     for i, out in enumerate((q_ref, k_ref, v_ref)):
@@ -640,24 +639,60 @@
     keep[:, columns] = (kept[:half].astype(F32) + arrived[:half].astype(F32)).astype(BF16)
 
 
+def fold_in(ref, row, value):
+    rows, width = value.shape[0], ref.shape[1]
+    more = value.shape[1] - width
+    blocks = width // more
+    size = rows // blocks
+    ref[row : row + rows, :] = value[:, :width]
+    for i in range(blocks):
+        ref[row + rows : row + rows + size, i * more : (i + 1) * more] = value[
+            i * size : (i + 1) * size, width:
+        ]
+
+
+def fold_out(ref, row, rows, columns):
+    width = ref.shape[1]
+    more = columns - width
+    blocks = width // more
+    size = rows // blocks
+    below = [
+        ref[row + rows : row + rows + size, i * more : (i + 1) * more] for i in range(blocks)
+    ]
+    return jnp.concatenate([ref[row : row + rows, :], jnp.concatenate(below, axis=0)], axis=1)
+
+
 def weight_add_body(plan, peers, me_ref, *refs):
-    keep_a, send_x, keep_b, send_y, keep_ca, keep_cb = refs[-6:]
-    ca, from_x, cb, from_y = refs[-10:-6]
+    keep_a, send_x, keep_b, send_y, keep_ca, keep_cb, keep_fa, keep_fb, keep_fc, send_z = refs[-10:]
+    ca, from_x, cb, from_y, fa, fa_there, fb, fb_there, fc, fc_there = refs[-20:-10]
     weights_into(plan, peers, me_ref, refs, [keep_a, send_x, keep_b, send_y])
     skip = keep_a.shape[0]
-    split_sum(need(ca, 0)[...], from_x[...], keep_ca, send_y, skip=skip)
-    split_sum(need(cb, 0)[...], from_y[...], keep_cb, send_x, skip=skip)
+    split_sum(ca[...], from_x[...], keep_ca, send_y, skip=skip)
+    split_sum(cb[...], from_y[...], keep_cb, send_x, skip=skip)
+    skip += keep_ca.shape[0]
+    split_sum(fa[...], fa_there[...], keep_fa, send_z)
+    half = keep_fb.shape[0]
+    for f, there, keep, send in ((fb, fb_there, keep_fb, send_x), (fc, fc_there, keep_fc, send_y)):
+        total = f[...].astype(F32) + there[...].astype(F32)
+        keep[...] = total[:half].astype(BF16)
+        fold_in(send, skip, total[half:].astype(BF16))
 
 
 def add_both_body(
-    sa, sb, ca, cb, from_x, from_y,
-    keep_sa, keep_sb, send_x, send_y, keep_c, send_z,
+    sa, sb, ca, cb, fa, fb, fc, from_x, from_y, from_z,
+    keep_sa, keep_sb, send_x, send_y, keep_c, send_z, keep_f, send_w,
 ):
     skip, wide = sa.shape[0], ca.shape[1]
+    low = skip + ca.shape[0]
     split_sum(sa[...], from_x[:skip], keep_sa, send_y)
     split_sum(sb[...], from_y[:skip], keep_sb, send_x)
-    split_sum(ca[...], from_y[skip:], keep_c, send_z, slice(0, wide))
-    split_sum(cb[...], from_x[skip:], keep_c, send_z, slice(wide, 2 * wide))
+    split_sum(ca[...], from_y[skip:low], keep_c, send_z, slice(0, wide))
+    split_sum(cb[...], from_x[skip:low], keep_c, send_z, slice(wide, 2 * wide))
+    rows, columns = fa.shape[0], fa.shape[1]
+    split_sum(fa[...], from_z[...], keep_f, send_w, slice(0, columns))
+    for i, (f, ref) in enumerate(((fb, from_x), (fc, from_y))):
+        arrived = fold_out(ref, low, rows, columns)
+        split_sum(f[...], arrived, keep_f, send_w, slice((i + 1) * columns, (i + 2) * columns))
 
 
 def add_last_body(sa, sb, c, from_x, from_y, from_z, keep_s, send_z, keep_c, send_w):
@@ -705,9 +740,12 @@
         body = weight_add_body
         args += also
         keep_a, send_a, keep_b, send_b = outs
-        tall = shape((width // 2 + also[0].shape[0] // 2, total), BF16)
-        small = Far(shape((also[0].shape[0] // 2, also[0].shape[1]), BF16))
-        outs = [keep_a, tall, keep_b, tall, small, small]
+        cross, ff = also[0], also[4]
+        rows, more = cross.shape[0] // 2, ff.shape[0] // 2
+        tall = width // 2 + rows + more * ff.shape[1] // total
+        small, thin = Far(shape((rows, total), BF16)), Far(shape((more, ff.shape[1]), BF16))
+        outs = [keep_a, shape((tall, total), BF16), keep_b, shape((tall, total), BF16)]
+        outs += [small] * 2 + [thin] * 3 + [thin.array]
     return call(
         partial(body, tuple(plan), peers), outs, args, flops=flops, smem=(0,),
         after=after, weight=weight,
@@ -800,13 +838,6 @@
             self.halves = call(add_join_body, outs, self.pairs(), after=after, weight=LIGHT)
         self.send()
         return self.halves[0]
-
-    def finish(self, outs, moves, after=(), weight=LIGHT):
-        while self.place < len(self.orders[0]):
-            self.step()
-        return call(
-            partial(finish_body, moves), [Far(o) for o in outs], self.pairs(), after=after, weight=weight
-        )
 
 
 def local(
@@ -897,11 +928,11 @@
     other = swap(own)
 
     by_head = partial(Far, axis=0, count=heads)
-    x, n1_turned, sq, sk, sv, self_probs, self_mix, part_one = call(
+    x, x_far, n1_turned, sq, sk, sv, self_probs, self_mix, part_one = call(
         self_forward_body,
         [
-            Far(wide), Far(turned), Far(narrow), Far(narrow), Far(narrow), by_head(probs_shape),
-            Far(narrow), wide,
+            wide, Far(wide), Far(turned), Far(narrow), Far(narrow), Far(narrow),
+            by_head(probs_shape), Far(narrow), wide,
         ],
         [core_ref, own, other, gain_one, self_qkv, mask, bias, self_out],
         flops=8 * square + 8 * scores * HEAD_DIM,
@@ -916,12 +947,12 @@
         flops=4 * square,
         scratch=[pltpu.VMEM((rows, width), BF16)],
         smem=(0,),
-        after=[x],
+        after=[x_far],
     )
     h1, h1_far, n2_turned, cq, cross_probs, cross_mix, part_two = call(
         cross_forward_body,
         [wide32, Far(wide32), Far(turned), Far(narrow), by_head(probs_shape), Far(narrow), wide],
-        [part_one, part_there, Far(x), gain_two, cross_qkv, ck, mask, cv, cross_out],
+        [part_one, part_there, x, gain_two, cross_qkv, ck, mask, cv, cross_out],
         flops=4 * square + 8 * scores * HEAD_DIM,
         scratch=[pltpu.VMEM((rows, width), BF16)],
     )
@@ -941,9 +972,9 @@
     third = 2 * units // 3
     ff_sum = Sum(
         weight_halves(me_ref, peers, orders, [
-            [(Far(og_turned), [(act, 0, third)])],
+            [(og_turned, [(act, 0, third)])],
             [
-                (Far(og_turned), [(act, third, units)]),
+                (og_turned, [(act, third, units)]),
                 (n3_turned, [(d_pre, 0, 2 * third - units)]),
             ],
             [(n3_turned, [(d_pre, 2 * third - units, units)])],
@@ -1009,12 +1040,20 @@
     ]
     merged = bits == 4
     if merged:
-        ca, _, cb, _ = cross_sum.halves
-        keep_sa, send_x, keep_sb, send_y, keep_ca, keep_cb = weight_halves(
-            me_ref, peers, pair_orders, self_sides, weight=AFTER_SELF, after=[dgain2],
-            also=[ca, cross_sum.arrived[0], cb, cross_sum.arrived[1]],
+        ca, cb = cross_sum.halves[0::2]
+        fa, fb, fc = ff_sum.halves[0::2]
+        fa_there, fb_there, fc_there = ff_sum.arrived
+        keep_sa, send_x, keep_sb, send_y, keep_ca, keep_cb, keep_fa, keep_fb, keep_fc, send_z = (
+            weight_halves(
+                me_ref, peers, pair_orders, self_sides, weight=AFTER_SELF, after=[dgain2],
+                also=[
+                    ca, cross_sum.arrived[0], cb, cross_sum.arrived[1],
+                    fa, fa_there, fb, fb_there, fc, fc_there,
+                ],
+            )
         )
         from_x, from_y = neighbour(send_x, 0, peers), neighbour(send_y, 1, peers)
+        from_z = neighbour(send_z, 2, peers)
         self_token = keep_sa
     else:
         self_sum = Sum(
@@ -1024,80 +1063,70 @@
             pair_orders, peers,
         )
         self_token = self_sum.halves[0]
-    ff_token = self_token
-    if FF_FIRST:
-        ff_token = ff_sum.step(after=[self_token])
     [packed] = call(
         partial(last_body, peers),
         [shape((slots + peers * EXTRA, width), BF16)],
         [
-            core_ref, taken_wide, dn1_there, Far(dn1), Far(x), gain_one, Far(g1_own), dgain2, dgain3,
+            core_ref, taken_wide, dn1_there, Far(dn1), Far(x_far), gain_one, Far(g1_own), dgain2, dgain3,
             diag, jnp.asarray(bucket_hot, F32),
         ],
         smem=(0,),
-        after=[ff_token, Near(mem_back)],
+        after=[self_token, Near(mem_back)],
         weight=LIGHT,
     )
     back = exchange_rows(packed, peers)
     token = Near(packed)
     half = width // 8
+
+    def ff_finish(ff_pair, after):
+        return call(
+            partial(finish_body, ((0, None, [(units, 2 * units)]), (1, None, [(0, units)]))),
+            [Far(shape((block, units), F32))] * 2, ff_pair, after=after, weight=LAST_WEIGHT,
+        )
+
     if merged:
-        if not FF_FIRST:
-            token = ff_sum.step(after=[token])
-        wide_pair = columns * 4
-
-        def two():
-            keep_sa2, keep_sb2, send_x2, send_y2, keep_c, send_z = call(
-                add_both_body,
-                [Far(shape((2 * half, 2 * columns), BF16))] * 2
-                + [shape((2 * half, 2 * columns), BF16)] * 2
-                + [Far(shape((half, wide_pair), BF16)), shape((half, wide_pair), BF16)],
-                [keep_sa, keep_sb, keep_ca, keep_cb, from_x, from_y],
-                after=[token],
-                weight=LIGHT,
-            )
-            return keep_sa2, keep_sb2, keep_c, (
-                neighbour(send_x2, 0, peers), neighbour(send_y2, 1, peers), neighbour(send_z, 2, peers)
-            )
-
-        if TWO_FIRST:
-            keep_sa2, keep_sb2, keep_c, arrived_two = two()
-            token = ff_sum.step(after=[keep_sa2])
-        else:
-            token = ff_sum.step(after=[token])
-            keep_sa2, keep_sb2, keep_c, arrived_two = two()
-            token = keep_sa2
-        keep_s, send_z, keep_c, send_w = call(
-            add_last_body,
-            pieces(half, wide_pair) + pieces(half // 2, wide_pair),
-            [keep_sa2, keep_sb2, keep_c, *arrived_two],
+        pair, ff_wide = columns * 4, units * 2
+        narrow_pair = shape((2 * half, 2 * columns), BF16)
+        keep_sa, keep_sb, send_x, send_y, keep_c, send_z, keep_f, send_w = call(
+            add_both_body,
+            [Far(narrow_pair), Far(narrow_pair), narrow_pair, narrow_pair]
+            + pieces(half, pair)
+            + pieces(half // 2, ff_wide),
+            [*map(Far, (keep_sa, keep_sb, keep_ca, keep_cb, keep_fa, keep_fb, keep_fc)), from_x, from_y, from_z],
             after=[token],
             weight=LIGHT,
         )
+        ff_pair = [keep_f, neighbour(send_w, 3, peers)]
+        keep_s, send_z, keep_c, send_w = call(
+            add_last_body,
+            pieces(half, pair) + pieces(half // 2, pair),
+            [
+                Far(keep_sa), Far(keep_sb), Far(keep_c),
+                neighbour(send_x, 0, peers), neighbour(send_y, 1, peers),
+                neighbour(send_z, 2, peers),
+            ],
+            weight=LIGHT,
+        )
         cross_arrived, from_z = neighbour(send_w, 3, peers), neighbour(send_z, 2, peers)
+        ff_in_total, ff_out_total = ff_finish(ff_pair, [keep_s])
         keep_s, send_w = call(
-            add_split_body, pieces(half // 2, wide_pair), [keep_s, from_z], weight=LIGHT
+            add_split_body, pieces(half // 2, pair), [keep_s, from_z], after=[ff_in_total], weight=LIGHT
         )
         self_arrived = neighbour(send_w, 3, peers)
         cross_pair, self_pair = [keep_c, cross_arrived], [keep_s, self_arrived]
     else:
-        for group in (cross_sum, ff_sum, self_sum, cross_sum, ff_sum, self_sum):
-            token = group.step(after=[token])
-        for group in (cross_sum, self_sum):
+        for group in (cross_sum, ff_sum, self_sum):
             while group.place < bits:
                 group.step()
         cross_pair, self_pair = cross_sum.pairs(), self_sum.pairs()
-    ff_in_total, ff_out_total = ff_sum.finish(
-        [shape((block, units), F32), shape((block, units), F32)],
-        ((0, None, [(units, 2 * units)]), (1, None, [(0, units)])),
-        weight=LAST_WEIGHT,
-    )
+        ff_in_total, ff_out_total = ff_finish(ff_sum.pairs(), [])
+        keep_s = ff_in_total
     memory_grad = unpack(mem_back, sent)
     input_grad, small = call(
         partial(unpack_last_body, peers),
         [Far(half16), shape((8, width), F32)],
         [sent_wide, back],
-        after=[ff_in_total, memory_grad],
+        after=[keep_s, memory_grad],
         weight=LIGHT,
     )
     moves = ((0, None, [(0, columns)]),) + tuple(

time: 237 us -> 236 us (level)
  waiting for transfers between devices: 76.8 us -> 83.3 us
  local copies, waits for them, and re-layouts: 8.43 us -> 3.37 us
    ppermute x20 -> x18, waiting for transfers between devices: 41.8 us -> 48.5 us  [neighbour(): return lax.ppermute(values, 'dp', [(i, i ^ 1 << bit) for i in range(peers)])]
    unnamed x124 -> x98, local copies, waits for them, and re-layouts: 7.11 us -> 2.05 us
    ppermute x20 -> x18, starting transfers between devices: 24.7 us -> 24.1 us  [neighbour(): return lax.ppermute(values, 'dp', [(i, i ^ 1 << bit) for i in range(peers)])]
    pallas_call x26 -> x24, Pallas kernels: 101 us -> 101 us  [call(): pl.pallas_call(kernel, out_shape=[(pltpu.HBM if i in far_out else pltpu.V...]
  transfers between devices with their start and end apart: 31 -> 29, of which waited for: 12 -> 13; matrix products, arithmetic and copies ran while one was open for 0% -> 0% of each run, Pallas kernels for 33% -> 34%
where the time goes in v1:
time: 236 us; the launch traced here: 232 us
  Pallas kernels  101 us (43%)
  waiting for transfers between devices  83.3 us (35%)
  starting transfers between devices  42.7 us (18%)
  local copies, waits for them, and re-layouts  3.37 us (1%)
    pallas_call x24, Pallas kernels, call(): pl.pallas_call(kernel, out_shape=[(pltpu.HBM if i in far_out else pltpu.V...  101 us
    ppermute x18, waiting for transfers between devices, neighbour(): return lax.ppermute(values, 'dp', [(i, i ^ 1 << bit) for i in range(peers)])  48.5 us
    all_to_all x3, waiting for transfers between devices, exchange_rows(): lax.all_to_all(blocks, 'dp', split_axis=0, concat_axis=0, tiled=True)  30.3 us
    ppermute x18, starting transfers between devices, neighbour(): return lax.ppermute(values, 'dp', [(i, i ^ 1 << bit) for i in range(peers)])  24.1 us
    all_to_all x3, starting transfers between devices, exchange_rows(): lax.all_to_all(blocks, 'dp', split_axis=0, concat_axis=0, tiled=True)  17.1 us
  transfers between devices with their start and end apart: 29, of which 13 were waited for; matrix products, arithmetic and copies ran while one was open for 0% of the time, Pallas kernels for 34%

profile of v1, /device:TPU:0, one launch (start us, length us, event | category | flops | bytes accessed | tf_op | source)
XLA Modules:
  0.0 232.4 jit_solution(10746173758988960873)
XLA Ops:
  1.9 3.7 %shard_map.230 = (bf16[512,1536]{1,0:T(8,128)(2,1)}, s32[1,512]{1,0:T(1,128)}) custom-call(s32[16,16]{1,0:T(8,128)S(1)} %copy-done.32, s32[1]{0:T(128)} %bitcast.1.refs_1_.refs_0_, bf16[256,768]{1,0:T(8,128)(2,1)} %refs_2_.1, bf16[256,768]{1,0:T(8,128)(2,1)} %refs_3_.3), custom_call_target="tpu_custom_call" | custom-call | flops 30000001024 | tf_op jit(solution)/shard_map/pallas_call | solution.py:188
  5.6 8.0 %all-to-all-start = ((bf16[16,32,1536]{2,1,0:T(8,128)(2,1)}), bf16[16,32,1536]{2,1,0:T(8,128)(2,1)S(1)}, u32[]{:S(2)}, u32[]{:S(2)}) async-start(bf16[16,32,1536]{2,1,0:T(8,128)(2,1)} %bitcast.3), calls=%async_computation | async-start | bytes 3145728 | tf_op jit(solution)/shard_map/all_to_all | solution.py:795
  13.8 2.6 %shard_map.231 = (bf16[6,256,512]{2,1,0:T(8,128)(2,1)}, f32[512,512]{1,0:T(8,128)}, s32[1,512]{1,0:T(1,128)}, s32[1,640]{1,0:T(1,128)}, s32[1,640]{1,0:T(1,128)}) custom-call(s32[16,16]{1,0:T(8,128)S(1)} %copy-done.33, s32[1]{0:T(128)} %bitcast.1.refs_1_.refs_0_, f32[6,256]{1,0:T(8,128)S(1)} %convolution_bitcast_fusion.refs_2_, s32[1,512]{1,0:T(1,128)S(1)} %copy-done.34, ...), custom_call_target="tpu_custom_call" | custom-call | flops 30000001024 | tf_op jit(solution)/shard_map/pallas_call | solution.py:188
  17.7 30.3 %all-to-all-done = bf16[16,32,1536]{2,1,0:T(8,128)(2,1)S(1)} async-done(((bf16[16,32,1536]{2,1,0:T(8,128)(2,1)}), bf16[16,32,1536]{2,1,0:T(8,128)(2,1)S(1)}, u32[]{:S(2)}, u32[]{:S(2)}) %all-to-all-start) | async-done | bytes 1572896 | tf_op jit(solution)/shard_map/all_to_all | solution.py:795
  48.7 2.2 collective-permute-done.1.refs_2_
  50.9 7.7 %shard_map.234 = (bf16[512,768]{1,0:T(8,128)(2,1)S(1)}, bf16[512,768]{1,0:T(8,128)(2,1)}, bf16[768,512]{1,0:T(8,128)(2,1)}, bf16[512,384]{1,0:T(8,128)(2,1)}, bf...) custom-call(s32[1]{0:T(128)} %bitcast.refs_0_, ...), custom_call_target="tpu_custom_call" | custom-call | flops 30000001024 | tf_op jit(solution)/shard_map/pallas_call | solution.py:188
  61.1 7.3 %shard_map.236 = (f32[512,768]{1,0:T(8,128)S(1)}, f32[512,768]{1,0:T(8,128)}, bf16[768,512]{1,0:T(8,128)(2,1)}, bf16[512,384]{1,0:T(8,128)(2,1)}, bf16[6,512,512...) custom-call(bf16[512,768]{1,0:T(8,128)(2,1)S(1)} %get-tuple-element.119.refs_0_, ...), custom_call_target="tpu_custom_call" | custom-call | flops 30000001024 | tf_op jit(solution)/shard_map/pallas_call | solution.py:188
  68.7 2.1 collective-permute-done.3.refs_2_
  70.8 6.9 %shard_map.237 = (bf16[768,512]{1,0:T(8,128)(2,1)S(1)}, f32[512,768]{1,0:T(8,128)S(1)}, bf16[512,1536]{1,0:T(8,128)(2,1)S(1)}, bf16[512,1536]{1,0:T(8,128)(2,1)S...) custom-call(s32[1]{0:T(128)} %bitcast.refs_0_, bf16[512,768]{1,0:T(8,128)(2,1)S(1)} %get-tuple-element.124.refs_1_, ...), custom_call_target="tpu_custom_call" | custom-call | flops 30000001024 | tf_op jit(solution)/shard_map/pallas_call | solution.py:188
  77.9 5.2 %shard_map.238 = (bf16[384,1024]{1,0:T(8,128)(2,1)}, bf16[384,1024]{1,0:T(8,128)(2,1)}, bf16[384,1024]{1,0:T(8,128)(2,1)}, bf16[384,1024]{1,0:T(8,128)(2,1)}, bf...) custom-call(s32[1]{0:T(128)} %bitcast.1.refs_1_.refs_0_, bf16[768,512]{1,0:T(8,128)(2,1)S(1)} %copy-done.43, ...), custom_call_target="tpu_custom_call" | custom-call | flops 30000001024 | tf_op jit(solution)/shard_map/pallas_call | solution.py:188
  84.4 2.7 %collective-permute-start.7 = (bf16[384,1024]{1,0:T(8,128)(2,1)}, bf16[384,1024]{1,0:T(8,128)(2,1)}, u32[]{:S(2)}, u32[]{:S(2)}) collective-permute-start(bf16[384,1024]{1,0:T(8,128)(2,1)} %get-tuple-element.148), channel_id=1, source_target_pairs={{0,4},{2,6},{4,0},{6,2},{8,12},{10,14},{12,8},{14,10},{16,20},{18,... | collective-permute-start | bytes 2359304 | tf_op jit(solution)/shard_map/ppermute | solution.py:803
  87.1 4.0 %collective-permute-start.8 = (bf16[384,1024]{1,0:T(8,128)(2,1)}, bf16[384,1024]{1,0:T(8,128)(2,1)}, u32[]{:S(2)}, u32[]{:S(2)}) collective-permute-start(bf16[384,1024]{1,0:T(8,128)(2,1)} %get-tuple-element.150), channel_id=1, source_target_pairs={{0,8},{2,10},{4,12},{6,14},{8,0},{10,2},{12,4},{14,6},{16,24},{18,... | collective-permute-start | bytes 2359304 | tf_op jit(solution)/shard_map/ppermute | solution.py:803
  91.2 20.5 %shard_map.239 = (f32[512,768]{1,0:T(8,128)}, bf16[768,512]{1,0:T(8,128)(2,1)S(1)}, bf16[512,384]{1,0:T(8,128)(2,1)S(1)}, bf16[512,384]{1,0:T(8,128)(2,1)S(1)}, ...) custom-call(s32[1]{0:T(128)} %bitcast.refs_0_, ...), custom_call_target="tpu_custom_call" | custom-call | flops 30000001024 | tf_op jit(solution)/shard_map/pallas_call | solution.py:188
  111.9 3.7 %shard_map.240 = (bf16[384,768]{1,0:T(8,128)(2,1)}, bf16[384,768]{1,0:T(8,128)(2,1)}, bf16[384,768]{1,0:T(8,128)(2,1)}, bf16[384,768]{1,0:T(8,128)(2,1)}) custom-call(s32[1]{0:T(128)} %bitcast.1.refs_1_.refs_0_, bf16[768,512]{1,0:T(8,128)(2,1)S(1)} %get-tuple-element.152.refs_1_, bf16[512,384]{1,0:T(8,128)(2,1)S(1)} %copy-done.46, ...), custom_call_target="tpu_custom_call" | custom-call | flops 30000001024 | tf_op jit(solution)/shard_map/pallas_call | solution.py:188
  118.3 4.6 %all-to-all-start.1 = ((bf16[16,32,768]{2,1,0:T(8,128)(2,1)}), bf16[16,32,768]{2,1,0:T(8,128)(2,1)S(1)}, u32[]{:S(2)}, u32[]{:S(2)}) async-start(bf16[16,32,768]{2,1,0:T(8,128)(2,1)} %bitcast.5), calls=%async_computation.1 | async-start | bytes 1572864 | tf_op jit(solution)/shard_map/all_to_all | solution.py:795
  124.1 3.0 %shard_map.242 = (bf16[192,1024]{1,0:T(8,128)(2,1)}, bf16[192,1024]{1,0:T(8,128)(2,1)S(1)}, bf16[192,1024]{1,0:T(8,128)(2,1)}, bf16[192,1024]{1,0:T(8,128)(2,1)S...) custom-call(bf16[384,1024]{1,0:T(8,128)(2,1)S(1)} %copy-done.2, ...), custom_call_target="tpu_custom_call" | custom-call | flops 1000000 | tf_op jit(solution)/shard_map/pallas_call | solution.py:188
  127.1 2.0 collective-permute-start.12
  132.0 12.0 %shard_map.243 = (f32[256,768]{1,0:T(8,128)}, bf16[768,512]{1,0:T(8,128)(2,1)S(1)}, bf16[512,384]{1,0:T(8,128)(2,1)S(1)}, bf16[512,384]{1,0:T(8,128)(2,1)S(1)}, ...) custom-call(s32[1]{0:T(128)} %bitcast.refs_0_, ...), custom_call_target="tpu_custom_call" | custom-call | flops 30000001024 | tf_op jit(solution)/shard_map/pallas_call | solution.py:188
  144.2 4.7 %collective-permute-done.12.refs_12_ = bf16[192,1024]{1,0:T(8,128)(2,1)S(1)} collective-permute-done((bf16[192,1024]{1,0:T(8,128)(2,1)S(1)}, bf16[192,1024]{1,0:T(8,128)(2,1)S(1)}, u32[]{:S(2)}, u32[]{:S(2)}) %collective-permute-start.12) | collective-permute-done | bytes 393248 | tf_op jit(solution)/shard_map/ppermute | solution.py:803
  149.0 7.4 %shard_map.244 = (bf16[384,768]{1,0:T(8,128)(2,1)}, bf16[704,768]{1,0:T(8,128)(2,1)}, bf16[384,768]{1,0:T(8,128)(2,1)}, bf16[704,768]{1,0:T(8,128)(2,1)}, bf16[1...) custom-call(s32[1]{0:T(128)} %bitcast.1.refs_1_.refs_0_, ...), custom_call_target="tpu_custom_call" | custom-call | flops 3000000000 | tf_op jit(solution)/shard_map/pallas_call | solution.py:188
  158.1 4.2 %shard_map.245.refs_10_ = bf16[640,768]{1,0:T(8,128)(2,1)} custom-call(s32[1]{0:T(128)} %bitcast.refs_0_, s32[1,640]{1,0:T(1,128)S(1)} %copy-done.16, bf16[256,768]{1,0:T(8,128)(2,1)S(1)} %collective-permute-done.9.refs_2_, f32[256,768]{1,0:T(8,128)} %get-tuple-element.163.refs_3_, bf16[512,768]{1,0:T(8,128)(2,1)} %get-tuple-element.121.refs_4_, ...), custom_call_target="tpu_custom_call" | custom-call | flops 1000000 | tf_op jit(solution)/shard_map/pallas_call | solution.py:188
  162.3 4.4 %all-to-all-start.2 = ((bf16[16,40,768]{2,1,0:T(8,128)(2,1)}), bf16[16,40,768]{2,1,0:T(8,128)(2,1)S(1)}, u32[]{:S(2)}, u32[]{:S(2)}) async-start(bf16[16,40,768]{2,1,0:T(8,128)(2,1)} %bitcast.7), calls=%async_computation.2 | async-start | bytes 1966080 | tf_op jit(solution)/shard_map/all_to_all | solution.py:795
  166.7 1.9 collective-permute-start.17
  168.6 18.9 %collective-permute-done.17.refs_9_ = bf16[96,1024]{1,0:T(8,128)(2,1)S(1)} collective-permute-done((bf16[96,1024]{1,0:T(8,128)(2,1)S(1)}, bf16[96,1024]{1,0:T(8,128)(2,1)S(1)}, u32[]{:S(2)}, u32[]{:S(2)}) %collective-permute-start.17) | collective-permute-done | bytes 196640 | tf_op jit(solution)/shard_map/ppermute | solution.py:803
  187.5 3.6 %collective-permute-done.15.refs_7_ = bf16[704,768]{1,0:T(8,128)(2,1)S(1)} collective-permute-done((bf16[704,768]{1,0:T(8,128)(2,1)}, bf16[704,768]{1,0:T(8,128)(2,1)S(1)}, u32[]{:S(2)}, u32[]{:S(2)}) %collective-permute-start.15) | collective-permute-done | bytes 1081376 | tf_op jit(solution)/shard_map/ppermute | solution.py:803
  192.8 4.0 %shard_map.246 = (bf16[192,768]{1,0:T(8,128)(2,1)}, bf16[192,768]{1,0:T(8,128)(2,1)}, bf16[192,768]{1,0:T(8,128)(2,1)S(1)}, bf16[192,768]{1,0:T(8,128)(2,1)S(1)}...) custom-call(bf16[384,768]{1,0:T(8,128)(2,1)} %get-tuple-element.182., ...), custom_call_target="tpu_custom_call" | custom-call | flops 1000000 | tf_op jit(solution)/shard_map/pallas_call | solution.py:188
  197.3 4.0 %collective-permute-start.22 = (bf16[48,3072]{1,0:T(8,128)(2,1)S(1)}, bf16[48,3072]{1,0:T(8,128)(2,1)S(1)}, u32[]{:S(2)}, u32[]{:S(2)}) collective-permute-start(bf16[48,3072]{1,0:T(8,128)(2,1)S(1)} %get-tuple-element.202), channel_id=1, source_target_pairs={{0,16},{2,18},{4,20},{6,22},{8,24},{10,26},{12,28},{14,30},{16,0},... | collective-permute-start | bytes 884744 | tf_op jit(solution)/shard_map/ppermute | solution.py:803
  201.3 2.3 collective-permute-done.18.refs_3_
  203.7 4.7 %collective-permute-done.20.refs_5_ = bf16[96,1536]{1,0:T(8,128)(2,1)S(1)} collective-permute-done((bf16[96,1536]{1,0:T(8,128)(2,1)S(1)}, bf16[96,1536]{1,0:T(8,128)(2,1)S(1)}, u32[]{:S(2)}, u32[]{:S(2)}) %collective-permute-start.20) | collective-permute-done | bytes 294944 | tf_op jit(solution)/shard_map/ppermute | solution.py:803
  208.5 1.9 shard_map.247
  213.0 8.2 %collective-permute-done.21.refs_1_ = bf16[96,1536]{1,0:T(8,128)(2,1)S(1)} collective-permute-done((bf16[96,1536]{1,0:T(8,128)(2,1)S(1)}, bf16[96,1536]{1,0:T(8,128)(2,1)S(1)}, u32[]{:S(2)}, u32[]{:S(2)}) %collective-permute-start.21) | collective-permute-done | bytes 294944 | tf_op jit(solution)/shard_map/ppermute | solution.py:803
  225.9 4.2 %collective-permute-done.24.refs_1_ = bf16[48,1536]{1,0:T(8,128)(2,1)S(1)} collective-permute-done((bf16[48,1536]{1,0:T(8,128)(2,1)S(1)}, bf16[48,1536]{1,0:T(8,128)(2,1)S(1)}, u32[]{:S(2)}, u32[]{:S(2)}) %collective-permute-start.24) | collective-permute-done | bytes 147488 | tf_op jit(solution)/shard_map/ppermute | solution.py:803
  (156 shorter events, 27.6 us)
Async XLA Ops:
  0.7 15.8 %collective-permute-start = (bf16[256,768]{1,0:T(8,128)(2,1)}, bf16[256,768]{1,0:T(8,128)(2,1)S(1)}, u32[]{:S(2)}, u32[]{:S(2)}) collective-permute-start(bf16[256,768]{1,0:T(8,128)(2,1)} %refs_1_.1), channel_id=1, source_target_pairs={{0,1},{1,0},{2,3},{3,2},{4,5},{5,4},{6,7},{7,6},{8,9},{9,8},{10,11... | collective-permute-start | bytes 1179656 | tf_op jit(solution)/shard_map/ppermute | solution.py:799
  5.6 42.3 %all-to-all-start = ((bf16[16,32,1536]{2,1,0:T(8,128)(2,1)}), bf16[16,32,1536]{2,1,0:T(8,128)(2,1)S(1)}, u32[]{:S(2)}, u32[]{:S(2)}) async-start(bf16[16,32,1536]{2,1,0:T(8,128)(2,1)} %bitcast.3), calls=%async_computation | async-start | bytes 3145728 | tf_op jit(solution)/shard_map/all_to_all | solution.py:795
  16.4 31.5 %copy-start.18 = (s32[1,512]{1,0:T(1,128)S(1)}, s32[1,512]{1,0:T(1,128)}, u32[]{:S(2)}) copy-start(s32[1,512]{1,0:T(1,128)} %get-tuple-element.114.refs_0_) | copy-start | bytes 6148
  48.6 2.4 %collective-permute-start.1 = (bf16[256,1536]{1,0:T(8,128)(2,1)S(1)}, bf16[256,1536]{1,0:T(8,128)(2,1)S(1)}, u32[]{:S(2)}, u32[]{:S(2)}) collective-permute-start(bf16[256,1536]{1,0:T(8,128)(2,1)S(1)} %shard_map.233.refs_1_), channel_id=1, source_target_pairs={{0,1},{1,0},{2,3},{3,2},{4,5},{5,4},{6,7},{7,6},{8,9},{9,8},{10,11... | collective-permute-start | bytes 2359304 | tf_op jit(solution)/shard_map/ppermute | solution.py:799
  58.7 2.4 %collective-permute-start.2 = (bf16[512,768]{1,0:T(8,128)(2,1)S(1)}, bf16[512,768]{1,0:T(8,128)(2,1)S(1)}, u32[]{:S(2)}, u32[]{:S(2)}) collective-permute-start(bf16[512,768]{1,0:T(8,128)(2,1)S(1)} %get-tuple-element.119.refs_0_), channel_id=1, source_target_pairs={{0,1},{1,0},{2,3},{3,2},{4,5},{5,4},{6,7},{7,6},{8,9},{9,8},{10,11... | collective-permute-start | bytes 2359304 | tf_op jit(solution)/shard_map/ppermute | solution.py:799
  68.4 2.4 %collective-permute-start.3 = (bf16[512,768]{1,0:T(8,128)(2,1)S(1)}, bf16[512,768]{1,0:T(8,128)(2,1)S(1)}, u32[]{:S(2)}, u32[]{:S(2)}) collective-permute-start(bf16[512,768]{1,0:T(8,128)(2,1)S(1)} %get-tuple-element.124.refs_1_), channel_id=1, source_target_pairs={{0,1},{1,0},{2,3},{3,2},{4,5},{5,4},{6,7},{7,6},{8,9},{9,8},{10,11... | collective-permute-start | bytes 2359304 | tf_op jit(solution)/shard_map/ppermute | solution.py:799
  77.7 13.5 %collective-permute-start.4 = (bf16[768,768]{1,0:T(8,128)(2,1)S(1)}, bf16[768,768]{1,0:T(8,128)(2,1)S(1)}, u32[]{:S(2)}, u32[]{:S(2)}) collective-permute-start(bf16[768,768]{1,0:T(8,128)(2,1)S(1)} %get-tuple-element.127.refs_1_), channel_id=1, source_target_pairs={{0,1},{1,0},{2,3},{3,2},{4,5},{5,4},{6,7},{7,6},{8,9},{9,8},{10,11... | collective-permute-start | bytes 3538952 | tf_op jit(solution)/shard_map/ppermute | solution.py:799
  83.2 39.7 %collective-permute-start.6 = (bf16[384,1024]{1,0:T(8,128)(2,1)}, bf16[384,1024]{1,0:T(8,128)(2,1)}, u32[]{:S(2)}, u32[]{:S(2)}) collective-permute-start(bf16[384,1024]{1,0:T(8,128)(2,1)} %get-tuple-element.146), channel_id=1, source_target_pairs={{0,2},{2,0},{4,6},{6,4},{8,10},{10,8},{12,14},{14,12},{16,18},{18,... | collective-permute-start | bytes 2359304 | tf_op jit(solution)/shard_map/ppermute | solution.py:803
  84.4 38.5 %collective-permute-start.7 = (bf16[384,1024]{1,0:T(8,128)(2,1)}, bf16[384,1024]{1,0:T(8,128)(2,1)}, u32[]{:S(2)}, u32[]{:S(2)}) collective-permute-start(bf16[384,1024]{1,0:T(8,128)(2,1)} %get-tuple-element.148), channel_id=1, source_target_pairs={{0,4},{2,6},{4,0},{6,2},{8,12},{10,14},{12,8},{14,10},{16,20},{18,... | collective-permute-start | bytes 2359304 | tf_op jit(solution)/shard_map/ppermute | solution.py:803
  87.1 35.8 %collective-permute-start.8 = (bf16[384,1024]{1,0:T(8,128)(2,1)}, bf16[384,1024]{1,0:T(8,128)(2,1)}, u32[]{:S(2)}, u32[]{:S(2)}) collective-permute-start(bf16[384,1024]{1,0:T(8,128)(2,1)} %get-tuple-element.150), channel_id=1, source_target_pairs={{0,8},{2,10},{4,12},{6,14},{8,0},{10,2},{12,4},{14,6},{16,24},{18,... | collective-permute-start | bytes 2359304 | tf_op jit(solution)/shard_map/ppermute | solution.py:803
  91.2 20.7 %copy-start.42 = (bf16[768,512]{1,0:T(8,128)(2,1)S(1)}, bf16[768,512]{1,0:T(8,128)(2,1)}, u32[]{:S(2)}) copy-start(bf16[768,512]{1,0:T(8,128)(2,1)} %get-tuple-element.154.refs_3_) | copy-start | bytes 2359300
  91.2 20.7 %copy-start.44 = (bf16[768,512]{1,0:T(8,128)(2,1)S(1)}, bf16[768,512]{1,0:T(8,128)(2,1)}, u32[]{:S(2)}) copy-start(bf16[768,512]{1,0:T(8,128)(2,1)} %get-tuple-element.156.refs_5_) | copy-start | bytes 2359300
  111.7 4.7 %collective-permute-start.5 = (bf16[768,768]{1,0:T(8,128)(2,1)}, bf16[768,768]{1,0:T(8,128)(2,1)S(1)}, u32[]{:S(2)}, u32[]{:S(2)}) collective-permute-start(bf16[768,768]{1,0:T(8,128)(2,1)} %get-tuple-element.139.refs_1_), channel_id=1, source_target_pairs={{0,1},{1,0},{2,3},{3,2},{4,5},{5,4},{6,7},{7,6},{8,9},{9,8},{10,11... | collective-permute-start | bytes 3538952 | tf_op jit(solution)/shard_map/ppermute | solution.py:799
  115.6 28.5 %collective-permute-start.10 = (bf16[384,768]{1,0:T(8,128)(2,1)}, bf16[384,768]{1,0:T(8,128)(2,1)}, u32[]{:S(2)}, u32[]{:S(2)}) collective-permute-start(bf16[384,768]{1,0:T(8,128)(2,1)} %get-tuple-element.174), channel_id=1, source_target_pairs={{0,2},{2,0},{4,6},{6,4},{8,10},{10,8},{12,14},{14,12},{16,18},{18,... | collective-permute-start | bytes 1769480 | tf_op jit(solution)/shard_map/ppermute | solution.py:803
  116.4 27.7 %collective-permute-start.11 = (bf16[384,768]{1,0:T(8,128)(2,1)}, bf16[384,768]{1,0:T(8,128)(2,1)}, u32[]{:S(2)}, u32[]{:S(2)}) collective-permute-start(bf16[384,768]{1,0:T(8,128)(2,1)} %get-tuple-element.176), channel_id=1, source_target_pairs={{0,4},{2,6},{4,0},{6,2},{8,12},{10,14},{12,8},{14,10},{16,20},{18,... | collective-permute-start | bytes 1769480 | tf_op jit(solution)/shard_map/ppermute | solution.py:803
  118.3 39.8 %all-to-all-start.1 = ((bf16[16,32,768]{2,1,0:T(8,128)(2,1)}), bf16[16,32,768]{2,1,0:T(8,128)(2,1)S(1)}, u32[]{:S(2)}, u32[]{:S(2)}) async-start(bf16[16,32,768]{2,1,0:T(8,128)(2,1)} %bitcast.5), calls=%async_computation.1 | async-start | bytes 1572864 | tf_op jit(solution)/shard_map/all_to_all | solution.py:795
  127.1 21.8 %collective-permute-start.12 = (bf16[192,1024]{1,0:T(8,128)(2,1)S(1)}, bf16[192,1024]{1,0:T(8,128)(2,1)S(1)}, u32[]{:S(2)}, u32[]{:S(2)}) collective-permute-start(bf16[192,1024]{1,0:T(8,128)(2,1)S(1)} %get-tuple-element.177), channel_id=1, source_target_pairs={{0,4},{2,6},{4,0},{6,2},{8,12},{10,14},{12,8},{14,10},{16,20},{18,... | collective-permute-start | bytes 1179656 | tf_op jit(solution)/shard_map/ppermute | solution.py:803
  129.1 19.8 %collective-permute-start.13 = (bf16[192,1024]{1,0:T(8,128)(2,1)S(1)}, bf16[192,1024]{1,0:T(8,128)(2,1)S(1)}, u32[]{:S(2)}, u32[]{:S(2)}) collective-permute-start(bf16[192,1024]{1,0:T(8,128)(2,1)S(1)} %get-tuple-element.179), channel_id=1, source_target_pairs={{0,8},{2,10},{4,12},{6,14},{8,0},{10,2},{12,4},{14,6},{16,24},{18,... | collective-permute-start | bytes 1179656 | tf_op jit(solution)/shard_map/ppermute | solution.py:803
  130.5 18.4 %collective-permute-start.14 = (bf16[192,1024]{1,0:T(8,128)(2,1)S(1)}, bf16[192,1024]{1,0:T(8,128)(2,1)S(1)}, u32[]{:S(2)}, u32[]{:S(2)}) collective-permute-start(bf16[192,1024]{1,0:T(8,128)(2,1)S(1)} %get-tuple-element.181), channel_id=1, source_target_pairs={{0,2},{2,0},{4,6},{6,4},{8,10},{10,8},{12,14},{14,12},{16,18},{18,... | collective-permute-start | bytes 1179656 | tf_op jit(solution)/shard_map/ppermute | solution.py:803
  144.1 14.0 %collective-permute-start.9 = (bf16[256,768]{1,0:T(8,128)(2,1)S(1)}, bf16[256,768]{1,0:T(8,128)(2,1)S(1)}, u32[]{:S(2)}, u32[]{:S(2)}) collective-permute-start(bf16[256,768]{1,0:T(8,128)(2,1)S(1)} %get-tuple-element.162), channel_id=1, source_target_pairs={{0,1},{1,0},{2,3},{3,2},{4,5},{5,4},{6,7},{7,6},{8,9},{9,8},{10,11... | collective-permute-start | bytes 1179656 | tf_op jit(solution)/shard_map/ppermute | solution.py:799
  156.4 34.6 %collective-permute-start.15 = (bf16[704,768]{1,0:T(8,128)(2,1)}, bf16[704,768]{1,0:T(8,128)(2,1)S(1)}, u32[]{:S(2)}, u32[]{:S(2)}) collective-permute-start(bf16[704,768]{1,0:T(8,128)(2,1)} %get-tuple-element.190), channel_id=1, source_target_pairs={{0,2},{2,0},{4,6},{6,4},{8,10},{10,8},{12,14},{14,12},{16,18},{18,... | collective-permute-start | bytes 3244040 | tf_op jit(solution)/shard_map/ppermute | solution.py:803
  157.8 35.0 %collective-permute-start.16 = (bf16[704,768]{1,0:T(8,128)(2,1)}, bf16[704,768]{1,0:T(8,128)(2,1)}, u32[]{:S(2)}, u32[]{:S(2)}) collective-permute-start(bf16[704,768]{1,0:T(8,128)(2,1)} %get-tuple-element.191), channel_id=1, source_target_pairs={{0,4},{2,6},{4,0},{6,2},{8,12},{10,14},{12,8},{14,10},{16,20},{18,... | collective-permute-start | bytes 3244040 | tf_op jit(solution)/shard_map/ppermute | solution.py:803
  162.3 61.4 %all-to-all-start.2 = ((bf16[16,40,768]{2,1,0:T(8,128)(2,1)}), bf16[16,40,768]{2,1,0:T(8,128)(2,1)S(1)}, u32[]{:S(2)}, u32[]{:S(2)}) async-start(bf16[16,40,768]{2,1,0:T(8,128)(2,1)} %bitcast.7), calls=%async_computation.2 | async-start | bytes 1966080 | tf_op jit(solution)/shard_map/all_to_all | solution.py:795
  166.7 20.8 %collective-permute-start.17 = (bf16[96,1024]{1,0:T(8,128)(2,1)S(1)}, bf16[96,1024]{1,0:T(8,128)(2,1)S(1)}, u32[]{:S(2)}, u32[]{:S(2)}) collective-permute-start(bf16[96,1024]{1,0:T(8,128)(2,1)S(1)} %get-tuple-element.192), channel_id=1, source_target_pairs={{0,8},{2,10},{4,12},{6,14},{8,0},{10,2},{12,4},{14,6},{16,24},{18,... | collective-permute-start | bytes 589832 | tf_op jit(solution)/shard_map/ppermute | solution.py:803
  196.8 6.8 %collective-permute-start.18 = (bf16[192,768]{1,0:T(8,128)(2,1)S(1)}, bf16[192,768]{1,0:T(8,128)(2,1)S(1)}, u32[]{:S(2)}, u32[]{:S(2)}) collective-permute-start(bf16[192,768]{1,0:T(8,128)(2,1)S(1)} %get-tuple-element.196), channel_id=1, source_target_pairs={{0,2},{2,0},{4,6},{6,4},{8,10},{10,8},{12,14},{14,12},{16,18},{18,... | collective-permute-start | bytes 884744 | tf_op jit(solution)/shard_map/ppermute | solution.py:803
  197.0 6.7 %collective-permute-start.19 = (bf16[192,768]{1,0:T(8,128)(2,1)S(1)}, bf16[192,768]{1,0:T(8,128)(2,1)S(1)}, u32[]{:S(2)}, u32[]{:S(2)}) collective-permute-start(bf16[192,768]{1,0:T(8,128)(2,1)S(1)} %get-tuple-element.197), channel_id=1, source_target_pairs={{0,4},{2,6},{4,0},{6,2},{8,12},{10,14},{12,8},{14,10},{16,20},{18,... | collective-permute-start | bytes 884744 | tf_op jit(solution)/shard_map/ppermute | solution.py:803
  197.3 11.1 %collective-permute-start.20 = (bf16[96,1536]{1,0:T(8,128)(2,1)S(1)}, bf16[96,1536]{1,0:T(8,128)(2,1)S(1)}, u32[]{:S(2)}, u32[]{:S(2)}) collective-permute-start(bf16[96,1536]{1,0:T(8,128)(2,1)S(1)} %get-tuple-element.198), channel_id=1, source_target_pairs={{0,8},{2,10},{4,12},{6,14},{8,0},{10,2},{12,4},{14,6},{16,24},{18,... | collective-permute-start | bytes 884744 | tf_op jit(solution)/shard_map/ppermute | solution.py:803
  197.3 14.8 %collective-permute-start.22 = (bf16[48,3072]{1,0:T(8,128)(2,1)S(1)}, bf16[48,3072]{1,0:T(8,128)(2,1)S(1)}, u32[]{:S(2)}, u32[]{:S(2)}) collective-permute-start(bf16[48,3072]{1,0:T(8,128)(2,1)S(1)} %get-tuple-element.202), channel_id=1, source_target_pairs={{0,16},{2,18},{4,20},{6,22},{8,24},{10,26},{12,28},{14,30},{16,0},... | collective-permute-start | bytes 884744 | tf_op jit(solution)/shard_map/ppermute | solution.py:803
  210.4 14.7 %collective-permute-start.25 = (bf16[48,1536]{1,0:T(8,128)(2,1)S(1)}, bf16[48,1536]{1,0:T(8,128)(2,1)S(1)}, u32[]{:S(2)}, u32[]{:S(2)}) collective-permute-start(bf16[48,1536]{1,0:T(8,128)(2,1)S(1)} %get-tuple-element.209), channel_id=1, source_target_pairs={{0,16},{2,18},{4,20},{6,22},{8,24},{10,26},{12,28},{14,30},{16,0},... | collective-permute-start | bytes 442376 | tf_op jit(solution)/shard_map/ppermute | solution.py:803
  210.5 10.8 %collective-permute-start.21 = (bf16[96,1536]{1,0:T(8,128)(2,1)S(1)}, bf16[96,1536]{1,0:T(8,128)(2,1)S(1)}, u32[]{:S(2)}, u32[]{:S(2)}) collective-permute-start(bf16[96,1536]{1,0:T(8,128)(2,1)S(1)} %get-tuple-element.200), channel_id=1, source_target_pairs={{0,8},{2,10},{4,12},{6,14},{8,0},{10,2},{12,4},{14,6},{16,24},{18,... | collective-permute-start | bytes 884744 | tf_op jit(solution)/shard_map/ppermute | solution.py:803
  222.0 8.1 %collective-permute-start.24 = (bf16[48,1536]{1,0:T(8,128)(2,1)S(1)}, bf16[48,1536]{1,0:T(8,128)(2,1)S(1)}, u32[]{:S(2)}, u32[]{:S(2)}) collective-permute-start(bf16[48,1536]{1,0:T(8,128)(2,1)S(1)} %get-tuple-element.207), channel_id=1, source_target_pairs={{0,16},{2,18},{4,20},{6,22},{8,24},{10,26},{12,28},{14,30},{16,0},... | collective-permute-start | bytes 442376 | tf_op jit(solution)/shard_map/ppermute | solution.py:803
  225.1 5.8 %collective-permute-start.23 = (f32[8,768]{1,0:T(8,128)S(1)}, f32[8,768]{1,0:T(8,128)S(1)}, u32[]{:S(2)}, u32[]{:S(2)}) collective-permute-start(f32[8,768]{1,0:T(8,128)S(1)} %get-tuple-element.206), channel_id=1, source_target_pairs={{0,1},{1,0},{2,3},{3,2},{4,5},{5,4},{6,7},{7,6},{8,9},{9,8},{10,11... | collective-permute-start | bytes 73736 | tf_op jit(solution)/shard_map/ppermute | solution.py:799
  (46 other events, 404.9 us)
